TPU v7x, 32 devices: a whole 2x2x4 slice. The times are simulated.
32 devices in a mesh: dp: 8 (over z, y), cent: 4 (over x, core).
Axes of the slice: x: 2, y: 2, z: 4, core: 2. Of those that a mesh axis runs over, the one named last changes fastest.
Arguments:
- clip_data: bfloat16 [4096, 4, 16, 192], P(('dp', 'cent')), may hold values from -6 to 6
- frame_counts: int32 [32, 128], P(('dp', 'cent')), may hold values from 1 to 4, 320 in all within a row
- send_list: int32 [32, 128], P(('dp', 'cent')), may hold values from 0 to 127, each once within a row
- cluster_ids: int32 [32, 128], P(('dp', 'cent')), may hold values from 0 to 37531, as said below
- expand_weight: bfloat16 [2, 192, 432], replicated, may hold values from -0.4375 to 0.4375
- depth_kernel: bfloat16 [2, 27, 432], replicated, may hold values from -1.25 to 1.25
- reduce_weight: bfloat16 [2, 432, 192], replicated, may hold values from -0.3125 to 0.3125
- head_weight: bfloat16 [192, 1024], replicated, may hold values from -0.4375 to 0.4375
- centroids: bfloat16 [50000, 1024], P('cent'), may hold values from -6 to 6
Outputs:
- embeddings: bfloat16 [4096, 1024], P(('dp', 'cent'))
- nearest: float32 [4096], P(('dp', 'cent'))
- own_sim: float32 [4096], P(('dp', 'cent'))
- peer_sim: float32 [4096], P(('dp', 'cent'))
Inputs may be any that keep to these rules, and one draw needn't show every extreme that they name: `cluster_ids`: cluster id q is owned by the device with dp index (q % 12500) % 8 and cent index q // 12500. The clips of one device name at most 16 clusters of one owner, and in every draw one owner gets exactly 16 from every device. Only ids with q % 12500 < 32 occur.
All inputs are finite; a program needn't handle non-finite values.
Results may differ from a plain program's by a relative error of at most 0.014.
Values may be sent and summed in bfloat16 or wider, within the bound.
A program may use at most 128 MiB of HBM per device.

v0:
```python
import jax
import jax.numpy as jnp
from jax import lax
from jax.sharding import PartitionSpec as P

SIDE = 4


def depthwise(hidden, kernel):
    frame_count = hidden.shape[1]
    padded = jnp.pad(hidden, ((0, 0), (1, 1), (1, 1), (1, 1), (0, 0)))
    accumulated = jnp.zeros_like(hidden)
    for shift_t in range(3):
        for shift_y in range(3):
            for shift_x in range(3):
                accumulated = (
                    accumulated
                    + kernel[9 * shift_t + 3 * shift_y + shift_x]
                    * padded[
                        :,
                        shift_t : shift_t + frame_count,
                        shift_y : shift_y + SIDE,
                        shift_x : shift_x + SIDE,
                        :,
                    ]
                )
    return accumulated


def embed_clips(clip_block, length_values, expand_weight, depth_kernel, reduce_weight, head_weight):
    clip_count, frame_count, positions, channels = clip_block.shape
    frame_mask = (
        jnp.arange(frame_count, dtype=jnp.float32)[None, :] < length_values[:, None]
    ).astype(jnp.float32)
    mask_four = frame_mask[:, :, None, None]
    features = clip_block * mask_four.astype(jnp.bfloat16)
    for layer_index in range(expand_weight.shape[0]):
        hidden = jax.nn.relu(
            jnp.dot(
                features.reshape(-1, channels),
                expand_weight[layer_index],
                preferred_element_type=jnp.float32,
            )
        )
        expanded = hidden.shape[-1]
        hidden = (
            hidden.reshape(clip_count, frame_count, SIDE, SIDE, expanded)
            * frame_mask[:, :, None, None, None]
        )
        mixed = depthwise(hidden, depth_kernel[layer_index].astype(jnp.float32))
        activated = (mixed * jax.nn.sigmoid(mixed)).astype(jnp.bfloat16)
        branch = jnp.dot(
            activated.reshape(-1, expanded),
            reduce_weight[layer_index],
            preferred_element_type=jnp.float32,
        )
        branch = branch.reshape(clip_count, frame_count, positions, channels)
        features = (features.astype(jnp.float32) + branch * mask_four).astype(jnp.bfloat16)
    pooled = (
        jnp.sum(features.astype(jnp.float32), axis=(1, 2)) / (length_values * positions)[:, None]
    ).astype(jnp.bfloat16)
    projected = jnp.dot(pooled, head_weight, preferred_element_type=jnp.float32)
    return (
        projected * lax.rsqrt(jnp.sum(projected * projected, axis=1, keepdims=True) + 1e-06)
    ).astype(jnp.bfloat16)


def local(
    clip_data,
    frame_counts,
    send_list,
    cluster_ids,
    expand_weight,
    depth_kernel,
    reduce_weight,
    head_weight,
    centroids,
):
    n_dp = lax.axis_size("dp")
    n_cent = lax.axis_size("cent")
    clip_count = clip_data.shape[0]
    per_peer = clip_count // n_dp
    destination = send_list[0]
    length_list = frame_counts[0]
    rest_shape = clip_data.shape[1:]

    def embed_pair(group_pair):
        return embed_clips(
            group_pair[0],
            group_pair[1].astype(jnp.float32),
            expand_weight,
            depth_kernel,
            reduce_weight,
            head_weight,
        )

    local_vectors = lax.map(
        embed_pair,
        (
            clip_data.reshape((per_peer, n_dp) + rest_shape),
            length_list.astype(jnp.bfloat16).reshape(per_peer, n_dp),
        ),
    )
    local_vectors = local_vectors.reshape(clip_count, -1)
    vector_buffer = (
        jnp.zeros_like(local_vectors).at[destination].set(local_vectors).reshape(per_peer, n_dp, -1)
    )
    vectors = lax.all_to_all(vector_buffer, "dp", split_axis=1, concat_axis=1, tiled=True).reshape(
        clip_count, -1
    )
    panel_size = centroids.shape[0]
    panel_blocks = centroids.reshape(5, panel_size // 5, -1)
    block_rows = lax.all_gather(vectors, "cent", axis=0, tiled=True)

    def visit(running, panel_block):
        scores = jnp.einsum(
            "rd,kd->rk", block_rows, panel_block, preferred_element_type=jnp.float32
        )
        return (jnp.maximum(running, jnp.max(scores, axis=1)), None)

    result, unused = lax.scan(
        visit, jnp.full((block_rows.shape[0],), -jnp.inf, jnp.float32), panel_blocks
    )
    all_best = lax.pmax(result, "cent")
    nearest = lax.dynamic_slice_in_dim(all_best, lax.axis_index("cent") * clip_count, clip_count)
    owner_total = n_dp * n_cent
    capacity = max(2, 4 * clip_count // owner_total)
    given = cluster_ids[0]
    panel_index = given % panel_size
    target = panel_index % n_dp * n_cent + given // panel_size
    slot_list = jnp.arange(clip_count, dtype=jnp.int32)
    earlier = (target[:, None] == target[None, :]) & (slot_list[None, :] < slot_list[:, None])
    position = jnp.sum(earlier.astype(jnp.int32), axis=1)
    width_d = vectors.shape[1]
    send_vectors = (
        jnp.zeros((owner_total, capacity, width_d), jnp.bfloat16).at[target, position].set(vectors)
    )
    label_rows = jnp.stack(
        [panel_index // 64, panel_index % 64, jnp.ones_like(panel_index)], axis=1
    ).astype(jnp.bfloat16)
    labels = (
        jnp.zeros((owner_total, capacity, 3), jnp.bfloat16).at[target, position].set(label_rows)
    )
    arrived_vectors, arrived_labels = (
        lax.all_to_all(send_vectors, ("dp", "cent"), split_axis=0, concat_axis=0, tiled=True),
        lax.all_to_all(labels, ("dp", "cent"), split_axis=0, concat_axis=0, tiled=True),
    )
    slot_total = owner_total * capacity
    member_vectors = arrived_vectors.reshape(slot_total, width_d)
    label_values = arrived_labels.reshape(slot_total, 3).astype(jnp.float32)
    row_index = (label_values[:, 0] * 64.0 + label_values[:, 1]).astype(jnp.int32)
    filled = label_values[:, 2] > 0.5
    centre_rows = centroids[row_index]
    own_values = jnp.sum(
        member_vectors.astype(jnp.float32) * centre_rows.astype(jnp.float32), axis=1
    )
    own_values = jnp.where(filled, own_values, 0.0)
    similarity = jnp.einsum(
        "rd,td->rt", member_vectors, member_vectors, preferred_element_type=jnp.float32
    )
    slots = jnp.arange(slot_total, dtype=jnp.int32)
    same_cluster = (
        (row_index[:, None] == row_index[None, :])
        & filled[:, None]
        & filled[None, :]
        & (slots[:, None] != slots[None, :])
    )
    peer_values = jnp.max(jnp.where(same_cluster, similarity, -1.0), axis=1)
    own_values, peer_values = (
        own_values.reshape(owner_total, capacity),
        peer_values.reshape(owner_total, capacity),
    )
    back_own, back_peer = (
        lax.all_to_all(own_values, ("dp", "cent"), split_axis=0, concat_axis=0, tiled=True),
        lax.all_to_all(peer_values, ("dp", "cent"), split_axis=0, concat_axis=0, tiled=True),
    )
    own_sim = back_own[target, position]
    peer_sim = back_peer[target, position]
    return (vectors, nearest, own_sim, peer_sim)


def solution(mesh):
    placed = (
        P(("dp", "cent"), None, None, None),
        P(("dp", "cent"), None),
        P(("dp", "cent"), None),
        P(("dp", "cent"), None),
        P(),
        P(),
        P(),
        P(),
        P("cent", None),
    )
    return jax.shard_map(
        local,
        mesh=mesh,
        in_specs=placed,
        out_specs=(
            P(("dp", "cent"), None),
            P(("dp", "cent")),
            P(("dp", "cent")),
            P(("dp", "cent")),
        ),
        check_vma=False,
    )
```

profile of v0, /device:TPU:0, one launch (start us, length us, event | category | flops | bytes accessed | tf_op | source)
XLA Modules:
  0.0 505.9 jit_solution(8319798606932235426)
XLA Ops:
  8.5 7.8 %copy.60 = bf16[128,4,16,192]{3,2,1,0:T(8,128)(2,1)} copy(bf16[128,4,16,192]{0,3,2,1:T(8,128)(2,1)} %param.13) | data formatting | bytes 6291456 | tf_op args[0]
  16.4 334.8 %while.23 = (s32[]{:T(128)}, bf16[16,8,1024]{2,1,0:T(8,128)(2,1)S(1)}, bf16[16,8,4,16,192]{4,3,2,1,0:T(8,128)(2,1)}, bf16[16,8]{1,0:T(8,128)(2,1)S(1)}, bf16[2,2...) while((s32[]{:T(128)}, ...), condition=%wide.region_3.4_spmd, body=%wide.region_0.3_spmd.sunk | while | flops 370663808 | bytes 23793328 | solution.py:97
  29.2 7.0 %fusion.208 = bf16[8,4,4,4,432]{4,3,2,1,0:T(4,128)(2,1)S(1)} fusion(f32[8,4,4,4,432]{4,3,2,1,0:T(4,128)S(1)} %broadcast_multiply_fusion.8, f32[432]{0:T(512)S(1)} %bitcast.362, f32[432]{0:T(512)S(1)} %bitcast.363, f32[432]{0:T(512)S(1)} %bitcast.364, f32[432]{0:T(512)S(1)} %bitcast.365, f32[432]{0:T(512)S(1)} %bitcast.366, f32[432]{0:T(512)S(1)} %bitcast.367, ...), kind=kLoop, calls=%fused_computation.175.clone.1 | loop fusion | flops 12828672 | bytes 1373760 | tf_op jit(solution)/shard_map/while/body/eval_jaxpr/convert_element_type | solution.py:51
  50.1 7.0 %fusion.208 = bf16[8,4,4,4,432]{4,3,2,1,0:T(4,128)(2,1)S(1)} fusion(f32[8,4,4,4,432]{4,3,2,1,0:T(4,128)S(1)} %broadcast_multiply_fusion.8, f32[432]{0:T(512)S(1)} %bitcast.362, f32[432]{0:T(512)S(1)} %bitcast.363, f32[432]{0:T(512)S(1)} %bitcast.364, f32[432]{0:T(512)S(1)} %bitcast.365, f32[432]{0:T(512)S(1)} %bitcast.366, f32[432]{0:T(512)S(1)} %bitcast.367, ...), kind=kLoop, calls=%fused_computation.175.clone.1 | loop fusion | flops 12828672 | bytes 1373760 | tf_op jit(solution)/shard_map/while/body/eval_jaxpr/convert_element_type | solution.py:51
  71.1 7.0 %fusion.208 = bf16[8,4,4,4,432]{4,3,2,1,0:T(4,128)(2,1)S(1)} fusion(f32[8,4,4,4,432]{4,3,2,1,0:T(4,128)S(1)} %broadcast_multiply_fusion.8, f32[432]{0:T(512)S(1)} %bitcast.362, f32[432]{0:T(512)S(1)} %bitcast.363, f32[432]{0:T(512)S(1)} %bitcast.364, f32[432]{0:T(512)S(1)} %bitcast.365, f32[432]{0:T(512)S(1)} %bitcast.366, f32[432]{0:T(512)S(1)} %bitcast.367, ...), kind=kLoop, calls=%fused_computation.175.clone.1 | loop fusion | flops 12828672 | bytes 1373760 | tf_op jit(solution)/shard_map/while/body/eval_jaxpr/convert_element_type | solution.py:51
  92.0 7.0 %fusion.208 = bf16[8,4,4,4,432]{4,3,2,1,0:T(4,128)(2,1)S(1)} fusion(f32[8,4,4,4,432]{4,3,2,1,0:T(4,128)S(1)} %broadcast_multiply_fusion.8, f32[432]{0:T(512)S(1)} %bitcast.362, f32[432]{0:T(512)S(1)} %bitcast.363, f32[432]{0:T(512)S(1)} %bitcast.364, f32[432]{0:T(512)S(1)} %bitcast.365, f32[432]{0:T(512)S(1)} %bitcast.366, f32[432]{0:T(512)S(1)} %bitcast.367, ...), kind=kLoop, calls=%fused_computation.175.clone.1 | loop fusion | flops 12828672 | bytes 1373760 | tf_op jit(solution)/shard_map/while/body/eval_jaxpr/convert_element_type | solution.py:51
  112.9 7.0 %fusion.208 = bf16[8,4,4,4,432]{4,3,2,1,0:T(4,128)(2,1)S(1)} fusion(f32[8,4,4,4,432]{4,3,2,1,0:T(4,128)S(1)} %broadcast_multiply_fusion.8, f32[432]{0:T(512)S(1)} %bitcast.362, f32[432]{0:T(512)S(1)} %bitcast.363, f32[432]{0:T(512)S(1)} %bitcast.364, f32[432]{0:T(512)S(1)} %bitcast.365, f32[432]{0:T(512)S(1)} %bitcast.366, f32[432]{0:T(512)S(1)} %bitcast.367, ...), kind=kLoop, calls=%fused_computation.175.clone.1 | loop fusion | flops 12828672 | bytes 1373760 | tf_op jit(solution)/shard_map/while/body/eval_jaxpr/convert_element_type | solution.py:51
  133.8 7.0 %fusion.208 = bf16[8,4,4,4,432]{4,3,2,1,0:T(4,128)(2,1)S(1)} fusion(f32[8,4,4,4,432]{4,3,2,1,0:T(4,128)S(1)} %broadcast_multiply_fusion.8, f32[432]{0:T(512)S(1)} %bitcast.362, f32[432]{0:T(512)S(1)} %bitcast.363, f32[432]{0:T(512)S(1)} %bitcast.364, f32[432]{0:T(512)S(1)} %bitcast.365, f32[432]{0:T(512)S(1)} %bitcast.366, f32[432]{0:T(512)S(1)} %bitcast.367, ...), kind=kLoop, calls=%fused_computation.175.clone.1 | loop fusion | flops 12828672 | bytes 1373760 | tf_op jit(solution)/shard_map/while/body/eval_jaxpr/convert_element_type | solution.py:51
  154.8 7.0 %fusion.208 = bf16[8,4,4,4,432]{4,3,2,1,0:T(4,128)(2,1)S(1)} fusion(f32[8,4,4,4,432]{4,3,2,1,0:T(4,128)S(1)} %broadcast_multiply_fusion.8, f32[432]{0:T(512)S(1)} %bitcast.362, f32[432]{0:T(512)S(1)} %bitcast.363, f32[432]{0:T(512)S(1)} %bitcast.364, f32[432]{0:T(512)S(1)} %bitcast.365, f32[432]{0:T(512)S(1)} %bitcast.366, f32[432]{0:T(512)S(1)} %bitcast.367, ...), kind=kLoop, calls=%fused_computation.175.clone.1 | loop fusion | flops 12828672 | bytes 1373760 | tf_op jit(solution)/shard_map/while/body/eval_jaxpr/convert_element_type | solution.py:51
  175.7 7.0 %fusion.208 = bf16[8,4,4,4,432]{4,3,2,1,0:T(4,128)(2,1)S(1)} fusion(f32[8,4,4,4,432]{4,3,2,1,0:T(4,128)S(1)} %broadcast_multiply_fusion.8, f32[432]{0:T(512)S(1)} %bitcast.362, f32[432]{0:T(512)S(1)} %bitcast.363, f32[432]{0:T(512)S(1)} %bitcast.364, f32[432]{0:T(512)S(1)} %bitcast.365, f32[432]{0:T(512)S(1)} %bitcast.366, f32[432]{0:T(512)S(1)} %bitcast.367, ...), kind=kLoop, calls=%fused_computation.175.clone.1 | loop fusion | flops 12828672 | bytes 1373760 | tf_op jit(solution)/shard_map/while/body/eval_jaxpr/convert_element_type | solution.py:51
  196.6 7.0 %fusion.208 = bf16[8,4,4,4,432]{4,3,2,1,0:T(4,128)(2,1)S(1)} fusion(f32[8,4,4,4,432]{4,3,2,1,0:T(4,128)S(1)} %broadcast_multiply_fusion.8, f32[432]{0:T(512)S(1)} %bitcast.362, f32[432]{0:T(512)S(1)} %bitcast.363, f32[432]{0:T(512)S(1)} %bitcast.364, f32[432]{0:T(512)S(1)} %bitcast.365, f32[432]{0:T(512)S(1)} %bitcast.366, f32[432]{0:T(512)S(1)} %bitcast.367, ...), kind=kLoop, calls=%fused_computation.175.clone.1 | loop fusion | flops 12828672 | bytes 1373760 | tf_op jit(solution)/shard_map/while/body/eval_jaxpr/convert_element_type | solution.py:51
  217.5 7.0 %fusion.208 = bf16[8,4,4,4,432]{4,3,2,1,0:T(4,128)(2,1)S(1)} fusion(f32[8,4,4,4,432]{4,3,2,1,0:T(4,128)S(1)} %broadcast_multiply_fusion.8, f32[432]{0:T(512)S(1)} %bitcast.362, f32[432]{0:T(512)S(1)} %bitcast.363, f32[432]{0:T(512)S(1)} %bitcast.364, f32[432]{0:T(512)S(1)} %bitcast.365, f32[432]{0:T(512)S(1)} %bitcast.366, f32[432]{0:T(512)S(1)} %bitcast.367, ...), kind=kLoop, calls=%fused_computation.175.clone.1 | loop fusion | flops 12828672 | bytes 1373760 | tf_op jit(solution)/shard_map/while/body/eval_jaxpr/convert_element_type | solution.py:51
  238.5 7.0 %fusion.208 = bf16[8,4,4,4,432]{4,3,2,1,0:T(4,128)(2,1)S(1)} fusion(f32[8,4,4,4,432]{4,3,2,1,0:T(4,128)S(1)} %broadcast_multiply_fusion.8, f32[432]{0:T(512)S(1)} %bitcast.362, f32[432]{0:T(512)S(1)} %bitcast.363, f32[432]{0:T(512)S(1)} %bitcast.364, f32[432]{0:T(512)S(1)} %bitcast.365, f32[432]{0:T(512)S(1)} %bitcast.366, f32[432]{0:T(512)S(1)} %bitcast.367, ...), kind=kLoop, calls=%fused_computation.175.clone.1 | loop fusion | flops 12828672 | bytes 1373760 | tf_op jit(solution)/shard_map/while/body/eval_jaxpr/convert_element_type | solution.py:51
  259.4 7.0 %fusion.208 = bf16[8,4,4,4,432]{4,3,2,1,0:T(4,128)(2,1)S(1)} fusion(f32[8,4,4,4,432]{4,3,2,1,0:T(4,128)S(1)} %broadcast_multiply_fusion.8, f32[432]{0:T(512)S(1)} %bitcast.362, f32[432]{0:T(512)S(1)} %bitcast.363, f32[432]{0:T(512)S(1)} %bitcast.364, f32[432]{0:T(512)S(1)} %bitcast.365, f32[432]{0:T(512)S(1)} %bitcast.366, f32[432]{0:T(512)S(1)} %bitcast.367, ...), kind=kLoop, calls=%fused_computation.175.clone.1 | loop fusion | flops 12828672 | bytes 1373760 | tf_op jit(solution)/shard_map/while/body/eval_jaxpr/convert_element_type | solution.py:51
  280.3 7.0 %fusion.208 = bf16[8,4,4,4,432]{4,3,2,1,0:T(4,128)(2,1)S(1)} fusion(f32[8,4,4,4,432]{4,3,2,1,0:T(4,128)S(1)} %broadcast_multiply_fusion.8, f32[432]{0:T(512)S(1)} %bitcast.362, f32[432]{0:T(512)S(1)} %bitcast.363, f32[432]{0:T(512)S(1)} %bitcast.364, f32[432]{0:T(512)S(1)} %bitcast.365, f32[432]{0:T(512)S(1)} %bitcast.366, f32[432]{0:T(512)S(1)} %bitcast.367, ...), kind=kLoop, calls=%fused_computation.175.clone.1 | loop fusion | flops 12828672 | bytes 1373760 | tf_op jit(solution)/shard_map/while/body/eval_jaxpr/convert_element_type | solution.py:51
  301.2 7.0 %fusion.208 = bf16[8,4,4,4,432]{4,3,2,1,0:T(4,128)(2,1)S(1)} fusion(f32[8,4,4,4,432]{4,3,2,1,0:T(4,128)S(1)} %broadcast_multiply_fusion.8, f32[432]{0:T(512)S(1)} %bitcast.362, f32[432]{0:T(512)S(1)} %bitcast.363, f32[432]{0:T(512)S(1)} %bitcast.364, f32[432]{0:T(512)S(1)} %bitcast.365, f32[432]{0:T(512)S(1)} %bitcast.366, f32[432]{0:T(512)S(1)} %bitcast.367, ...), kind=kLoop, calls=%fused_computation.175.clone.1 | loop fusion | flops 12828672 | bytes 1373760 | tf_op jit(solution)/shard_map/while/body/eval_jaxpr/convert_element_type | solution.py:51
  322.2 7.0 %fusion.208 = bf16[8,4,4,4,432]{4,3,2,1,0:T(4,128)(2,1)S(1)} fusion(f32[8,4,4,4,432]{4,3,2,1,0:T(4,128)S(1)} %broadcast_multiply_fusion.8, f32[432]{0:T(512)S(1)} %bitcast.362, f32[432]{0:T(512)S(1)} %bitcast.363, f32[432]{0:T(512)S(1)} %bitcast.364, f32[432]{0:T(512)S(1)} %bitcast.365, f32[432]{0:T(512)S(1)} %bitcast.366, f32[432]{0:T(512)S(1)} %bitcast.367, ...), kind=kLoop, calls=%fused_computation.175.clone.1 | loop fusion | flops 12828672 | bytes 1373760 | tf_op jit(solution)/shard_map/while/body/eval_jaxpr/convert_element_type | solution.py:51
  343.1 7.0 %fusion.208 = bf16[8,4,4,4,432]{4,3,2,1,0:T(4,128)(2,1)S(1)} fusion(f32[8,4,4,4,432]{4,3,2,1,0:T(4,128)S(1)} %broadcast_multiply_fusion.8, f32[432]{0:T(512)S(1)} %bitcast.362, f32[432]{0:T(512)S(1)} %bitcast.363, f32[432]{0:T(512)S(1)} %bitcast.364, f32[432]{0:T(512)S(1)} %bitcast.365, f32[432]{0:T(512)S(1)} %bitcast.366, f32[432]{0:T(512)S(1)} %bitcast.367, ...), kind=kLoop, calls=%fused_computation.175.clone.1 | loop fusion | flops 12828672 | bytes 1373760 | tf_op jit(solution)/shard_map/while/body/eval_jaxpr/convert_element_type | solution.py:51
  353.4 7.3 %all-to-all-start = ((bf16[16,8,1024]{2,0,1:T(8,128)(2,1)}), bf16[16,8,1024]{2,0,1:T(8,128)(2,1)S(1)}, u32[]{:S(2)}, u32[]{:S(2)}) async-start(bf16[16,8,1024]{2,0,1:T(8,128)(2,1)} %copy.61), calls=%async_computation | async-start | bytes 524288 | tf_op jit(solution)/shard_map/all_to_all | solution.py:108
  378.3 18.6 %scatter_fusion.1 = bf16[32,16,1024]{2,1,0:T(8,128)(2,1)} fusion(bf16[32,16,1024]{2,1,0:T(8,128)(2,1)} %broadcast_in_dim.35, s32[128]{0:T(128)S(1)} %fusion.156, bf16[128,1024]{1,0:T(8,128)(2,1)S(1)} %bitcast.322), kind=kCustom, calls=%fused_computation.5 | custom fusion | bytes 787456 | tf_op jit(solution)/shard_map/scatter | solution.py:136
  403.5 24.8 %reshape.619 = bf16[5,2500,1024]{2,1,0:T(8,128)(2,1)} reshape(bf16[12500,1024]{1,0:T(8,128)(2,1)} %param.21) | data formatting | bytes 51200000 | tf_op jit(solution)/shard_map/reshape | solution.py:112
  428.7 14.3 %gather_fusion = bf16[512,1024]{1,0:T(8,128)(2,1)S(1)} fusion(bf16[12500,1024]{1,0:T(8,128)(2,1)} %param.21, s32[1024]{0:T(1024)S(1)} %pad_clamp_fusion), kind=kCustom, calls=%fused_computation | custom fusion | bytes 2099200 | tf_op jit(solution)/shard_map/gather | solution.py:153
  459.4 28.4 %while.24 = (s32[]{:T(128)}, f32[512]{0:T(512)S(1)}, bf16[5,2500,1024]{2,1,0:T(8,128)(2,1)}, bf16[512,1024]{1,0:T(8,128)(2,1)}, s32[]{:T(128)}, /*index=5*/s32[]{:T(128)}) while((s32[]{:T(128)}, f32[512]{0:T(512)S(1)}, bf16[5,2500,1024]{2,1,0:T(8,128)(2,1)}, bf16[512,1024]{1,0:T(8,128)(2,1)}, s32[]{:T(128)}, ...), condition=%wide.region_7.8_spmd.clone, body=%wide.region_5.7_spmd.clone.sunk | while | flops 2622720512 | bytes 6185051 | solution.py:121
  487.8 7.0 %pmax.7 = f32[512]{0:T(512)S(1)} all-reduce(f32[512]{0:T(512)S(1)} %get-tuple-element.128), channel_id=1, replica_groups=mesh['dp'=8,'cent'=4] {'cent'}, use_global_device_ids=true, to_apply=%region_8.9 | all-reduce | flops 512 | bytes 4096 | tf_op jit(solution)/shard_map/pmax | solution.py:124
  (595 shorter events, 296.2 us)
Async XLA Ops:
  7.2 9.2 %copy-start.2 = (bf16[2,27,432]{2,0,1:T(2,128)(2,1)S(1)}, bf16[2,27,432]{2,0,1:T(2,128)(2,1)}, u32[]{:S(2)}) copy-start(bf16[2,27,432]{2,0,1:T(2,128)(2,1)} %param.18) | copy-start | bytes 139972
  16.4 9.9 %copy-start.5 = (bf16[16,8]{1,0:T(8,128)(2,1)}, bf16[16,8]{1,0:T(8,128)(2,1)S(1)}, u32[]{:S(2)}) copy-start(bf16[16,8]{1,0:T(8,128)(2,1)S(1)} %get-tuple-element.466) | copy-start | bytes 772 | tf_op jit(solution)/shard_map/while
  37.3 9.9 %copy-start.5 = (bf16[16,8]{1,0:T(8,128)(2,1)}, bf16[16,8]{1,0:T(8,128)(2,1)S(1)}, u32[]{:S(2)}) copy-start(bf16[16,8]{1,0:T(8,128)(2,1)S(1)} %get-tuple-element.466) | copy-start | bytes 772 | tf_op jit(solution)/shard_map/while
  58.2 9.9 %copy-start.5 = (bf16[16,8]{1,0:T(8,128)(2,1)}, bf16[16,8]{1,0:T(8,128)(2,1)S(1)}, u32[]{:S(2)}) copy-start(bf16[16,8]{1,0:T(8,128)(2,1)S(1)} %get-tuple-element.466) | copy-start | bytes 772 | tf_op jit(solution)/shard_map/while
  79.2 9.9 %copy-start.5 = (bf16[16,8]{1,0:T(8,128)(2,1)}, bf16[16,8]{1,0:T(8,128)(2,1)S(1)}, u32[]{:S(2)}) copy-start(bf16[16,8]{1,0:T(8,128)(2,1)S(1)} %get-tuple-element.466) | copy-start | bytes 772 | tf_op jit(solution)/shard_map/while
  100.1 9.9 %copy-start.5 = (bf16[16,8]{1,0:T(8,128)(2,1)}, bf16[16,8]{1,0:T(8,128)(2,1)S(1)}, u32[]{:S(2)}) copy-start(bf16[16,8]{1,0:T(8,128)(2,1)S(1)} %get-tuple-element.466) | copy-start | bytes 772 | tf_op jit(solution)/shard_map/while
  121.0 9.9 %copy-start.5 = (bf16[16,8]{1,0:T(8,128)(2,1)}, bf16[16,8]{1,0:T(8,128)(2,1)S(1)}, u32[]{:S(2)}) copy-start(bf16[16,8]{1,0:T(8,128)(2,1)S(1)} %get-tuple-element.466) | copy-start | bytes 772 | tf_op jit(solution)/shard_map/while
  141.9 9.9 %copy-start.5 = (bf16[16,8]{1,0:T(8,128)(2,1)}, bf16[16,8]{1,0:T(8,128)(2,1)S(1)}, u32[]{:S(2)}) copy-start(bf16[16,8]{1,0:T(8,128)(2,1)S(1)} %get-tuple-element.466) | copy-start | bytes 772 | tf_op jit(solution)/shard_map/while
  162.9 9.9 %copy-start.5 = (bf16[16,8]{1,0:T(8,128)(2,1)}, bf16[16,8]{1,0:T(8,128)(2,1)S(1)}, u32[]{:S(2)}) copy-start(bf16[16,8]{1,0:T(8,128)(2,1)S(1)} %get-tuple-element.466) | copy-start | bytes 772 | tf_op jit(solution)/shard_map/while
  183.8 9.9 %copy-start.5 = (bf16[16,8]{1,0:T(8,128)(2,1)}, bf16[16,8]{1,0:T(8,128)(2,1)S(1)}, u32[]{:S(2)}) copy-start(bf16[16,8]{1,0:T(8,128)(2,1)S(1)} %get-tuple-element.466) | copy-start | bytes 772 | tf_op jit(solution)/shard_map/while
  204.7 9.9 %copy-start.5 = (bf16[16,8]{1,0:T(8,128)(2,1)}, bf16[16,8]{1,0:T(8,128)(2,1)S(1)}, u32[]{:S(2)}) copy-start(bf16[16,8]{1,0:T(8,128)(2,1)S(1)} %get-tuple-element.466) | copy-start | bytes 772 | tf_op jit(solution)/shard_map/while
  225.6 9.9 %copy-start.5 = (bf16[16,8]{1,0:T(8,128)(2,1)}, bf16[16,8]{1,0:T(8,128)(2,1)S(1)}, u32[]{:S(2)}) copy-start(bf16[16,8]{1,0:T(8,128)(2,1)S(1)} %get-tuple-element.466) | copy-start | bytes 772 | tf_op jit(solution)/shard_map/while
  246.6 9.9 %copy-start.5 = (bf16[16,8]{1,0:T(8,128)(2,1)}, bf16[16,8]{1,0:T(8,128)(2,1)S(1)}, u32[]{:S(2)}) copy-start(bf16[16,8]{1,0:T(8,128)(2,1)S(1)} %get-tuple-element.466) | copy-start | bytes 772 | tf_op jit(solution)/shard_map/while
  267.5 9.9 %copy-start.5 = (bf16[16,8]{1,0:T(8,128)(2,1)}, bf16[16,8]{1,0:T(8,128)(2,1)S(1)}, u32[]{:S(2)}) copy-start(bf16[16,8]{1,0:T(8,128)(2,1)S(1)} %get-tuple-element.466) | copy-start | bytes 772 | tf_op jit(solution)/shard_map/while
  288.4 9.9 %copy-start.5 = (bf16[16,8]{1,0:T(8,128)(2,1)}, bf16[16,8]{1,0:T(8,128)(2,1)S(1)}, u32[]{:S(2)}) copy-start(bf16[16,8]{1,0:T(8,128)(2,1)S(1)} %get-tuple-element.466) | copy-start | bytes 772 | tf_op jit(solution)/shard_map/while
  309.3 9.9 %copy-start.5 = (bf16[16,8]{1,0:T(8,128)(2,1)}, bf16[16,8]{1,0:T(8,128)(2,1)S(1)}, u32[]{:S(2)}) copy-start(bf16[16,8]{1,0:T(8,128)(2,1)S(1)} %get-tuple-element.466) | copy-start | bytes 772 | tf_op jit(solution)/shard_map/while
  330.3 9.9 %copy-start.5 = (bf16[16,8]{1,0:T(8,128)(2,1)}, bf16[16,8]{1,0:T(8,128)(2,1)S(1)}, u32[]{:S(2)}) copy-start(bf16[16,8]{1,0:T(8,128)(2,1)S(1)} %get-tuple-element.466) | copy-start | bytes 772 | tf_op jit(solution)/shard_map/while
  353.4 17.6 %all-to-all-start = ((bf16[16,8,1024]{2,0,1:T(8,128)(2,1)}), bf16[16,8,1024]{2,0,1:T(8,128)(2,1)S(1)}, u32[]{:S(2)}, u32[]{:S(2)}) async-start(bf16[16,8,1024]{2,0,1:T(8,128)(2,1)} %copy.61), calls=%async_computation | async-start | bytes 524288 | tf_op jit(solution)/shard_map/all_to_all | solution.py:108
  371.0 25.9 %all-to-all-start.1 = ((bf16[32,16,3]{1,2,0:T(4,128)(2,1)}), bf16[32,16,3]{1,2,0:T(4,128)(2,1)S(1)}, u32[]{:S(2)}, u32[]{:S(2)}) async-start(bf16[32,16,3]{1,2,0:T(4,128)(2,1)} %copy.64), calls=%async_computation.1 | async-start | bytes 65536 | tf_op jit(solution)/shard_map/all_to_all | solution.py:146
  377.2 25.7 %copy-start.3 = (bf16[16,8,1024]{2,1,0:T(8,128)(2,1)}, bf16[16,8,1024]{2,1,0:T(8,128)(2,1)S(1)}, u32[]{:S(2)}) copy-start(bf16[16,8,1024]{2,1,0:T(8,128)(2,1)S(1)} %copy.74) | copy-start | bytes 786436
  396.9 46.1 %all-to-all-start.2 = ((bf16[32,16,1024]{2,1,0:T(8,128)(2,1)}), bf16[32,16,1024]{2,1,0:T(8,128)(2,1)S(1)}, u32[]{:S(2)}, u32[]{:S(2)}) async-start(bf16[32,16,1024]{2,1,0:T(8,128)(2,1)} %scatter_fusion.1), calls=%async_computation.2 | async-start | bytes 2097152 | tf_op jit(solution)/shard_map/all_to_all | solution.py:145
  402.7 56.7 %all-gather.2.cloned.1.call-start = ((), (), s32[]{:S(2)}) async-start(), calls=%async_computation.5 | async-start | bytes 1310720 | tf_op jit(solution)/shard_map/all_gather | solution.py:113
  444.0 13.0 %all-to-all-start.3 = ((f32[32,1,16]{2,1,0:T(1,128)}), f32[32,1,16]{2,1,0:T(1,128)S(1)}, u32[]{:S(2)}, u32[]{:S(2)}) async-start(f32[32,1,16]{2,1,0:T(1,128)} %bitcast.87), calls=%async_computation.3 | async-start | bytes 32768 | tf_op jit(solution)/shard_map/all_to_all | solution.py:174
  456.9 40.3 %all-to-all-start.4 = ((f32[32,1,16]{2,1,0:T(1,128)}), f32[32,1,16]{2,1,0:T(1,128)S(1)}, u32[]{:S(2)}, u32[]{:S(2)}) async-start(f32[32,1,16]{2,1,0:T(1,128)} %bitcast.92), calls=%async_computation.4 | async-start | bytes 32768 | tf_op jit(solution)/shard_map/all_to_all | solution.py:175
  (67 other events, 531.2 us)
Sparse Core Ops, SparseCore 0:
  405.7 19.7 all-gather.1
where the time goes:
time: 508 us; the launch traced here: 506 us
  other arithmetic  253 us (50%)
  local copies, waits for them, and re-layouts  123 us (24%)
  matrix products  71 us (14%)
  starting transfers between devices  27.5 us (5%)
  between operations  14.3 us (3%)
  blocking collectives  7.05 us (1%)
  waiting for transfers between devices  6.1 us (1%)
    convert_element_type x32, other arithmetic, embed_clips(): activated = (mixed * jax.nn.sigmoid(mixed)).astype(jnp.bfloat16)  212 us
    dot_general x5, matrix products, visit(): jnp.einsum('rd,kd->rk', block_rows, panel_block, preferred_element_type=j...  28.2 us
    dot_general x32, matrix products, embed_clips(): jnp.dot(activated.reshape(-1, expanded), reduce_weight[layer_index], pref...  26.1 us
    reshape x1, local copies, waits for them, and re-layouts, local(): panel_blocks = centroids.reshape(5, panel_size // 5, -1)  24.8 us
    scatter x1, local copies, waits for them, and re-layouts, local(): jnp.zeros((owner_total, capacity, width_d), jnp.bfloat16)  18.6 us
    mul x16, other arithmetic, embed_clips(): features = clip_block * mask_four.astype(jnp.bfloat16)  16.8 us
    gather x1, local copies, waits for them, and re-layouts, local(): centre_rows = centroids[row_index]  14.3 us
    reshape x32, local copies, waits for them, and re-layouts, embed_clips(): hidden.reshape(clip_count, frame_count, SIDE, SIDE, expanded)  11 us
  transfers between devices with their start and end apart: 6, of which 1 were waited for; matrix products, arithmetic and copies ran while one was open for 20% of the time, Pallas kernels for 0%

commit v1 on v0

v1 whole, which is shorter than its diff:
```python
import functools

import jax
import jax.numpy as jnp
from jax import lax
from jax.experimental import pallas as pl
from jax.experimental.pallas import tpu as pltpu
from jax.sharding import PartitionSpec as P

SIDE = 4
GROUPS = 4
ROWS = 16
F32 = jnp.float32
BF16 = jnp.bfloat16


def embed_kernel(
    order_ref,
    most_ref,
    clip_ref,
    count_ref,
    place_ref,
    expand_ref,
    depth_ref,
    reduce_ref,
    head_ref,
    out_ref,
    arrived,
    x,
    hidden,
    activated,
    pooled,
    taps,
    sems,
):
    clips, frames, positions, channels = clip_ref.shape
    layers, tap_count, expanded = depth_ref.shape
    blocks = clips // ROWS
    flat = positions * ROWS

    def fetch(i, carry):
        pltpu.make_async_copy(
            clip_ref.at[order_ref[i]], arrived.at[i], sems.at[i // ROWS]
        ).start()
        return carry

    lax.fori_loop(0, clips, fetch, 0)

    for layer in range(layers):
        rows = depth_ref[layer].astype(F32)
        for t in range(tap_count):
            taps[layer, t] = jnp.broadcast_to(rows[t : t + 1], (ROWS, expanded)).astype(BF16)

    to_row = lax.broadcasted_iota(jnp.int32, (flat, flat), 0)
    from_row = lax.broadcasted_iota(jnp.int32, (flat, flat), 1)
    turn = jnp.where(
        from_row == (to_row % ROWS) * positions + to_row // ROWS, 1.0, 0.0
    ).astype(BF16)
    lanes = [(at, min(at + 128, expanded)) for at in range(0, expanded, 128)]

    def convolve(layer, f, shifts):
        for lo, hi in lanes:
            for y in range(SIDE):
                sums = [None] * SIDE
                for a in shifts:
                    for b in range(3):
                        if not 0 <= y + b - 1 < SIDE:
                            continue
                        line = [
                            hidden[f + a - 1, (y + b - 1) * SIDE + z, :, lo:hi]
                            for z in range(SIDE)
                        ]
                        weights = [taps[layer, 9 * a + 3 * b + g, :, lo:hi] for g in range(3)]
                        for z in range(SIDE):
                            for g in range(3):
                                if 0 <= z + g - 1 < SIDE:
                                    term = weights[g] * line[z + g - 1]
                                    sums[z] = term if sums[z] is None else sums[z] + term
                for z in range(SIDE):
                    half = 0.5 * sums[z].astype(F32)
                    activated[y * SIDE + z, :, lo:hi] = (half + half * jnp.tanh(half)).astype(BF16)

    def block(b, carry):
        most = most_ref[b]
        first = pl.multiple_of(b * ROWS, ROWS)
        pltpu.make_async_copy(
            clip_ref.at[pl.ds(0, ROWS)], arrived.at[pl.ds(first, ROWS)], sems.at[b]
        ).wait()
        counts = count_ref[pl.ds(first, ROWS), :]

        def mask(f, width):
            wide = jnp.broadcast_to(counts, (ROWS, width))
            return jnp.where(wide > f.astype(F32), 1.0, 0.0)

        def load(f, carry):
            raw = arrived[pl.ds(first, ROWS), f].reshape(flat, channels)
            turned = jnp.dot(turn, raw, preferred_element_type=F32)
            x[f] = (turned.reshape(positions, ROWS, channels) * mask(f, channels)[None]).astype(BF16)
            return carry

        lax.fori_loop(0, most, load, 0)

        def layer_step(layer, carry):
            def expand(f, carry):
                wide = jnp.dot(
                    x[f].reshape(flat, channels), expand_ref[layer], preferred_element_type=F32
                )
                wide = jnp.maximum(wide, 0.0).astype(BF16).reshape(positions, ROWS, expanded)
                hidden[f] = wide * mask(f, expanded).astype(BF16)[None]
                return carry

            lax.fori_loop(0, most, expand, 0)

            def mix(f, carry):
                has_last, has_next = f > 0, f < most - 1
                for last in (False, True):
                    for following in (False, True):
                        shifts = ([0] if last else []) + [1] + ([2] if following else [])
                        chosen = jnp.logical_and(has_last == last, has_next == following)
                        pl.when(chosen)(functools.partial(convolve, layer, f, shifts))
                branch = jnp.dot(
                    activated[...].reshape(flat, expanded),
                    reduce_ref[layer],
                    preferred_element_type=F32,
                ).reshape(positions, ROWS, channels)
                x[f] = (x[f].astype(F32) + branch * mask(f, channels)[None]).astype(BF16)
                return carry

            lax.fori_loop(0, most, mix, 0)
            return carry

        lax.fori_loop(0, layers, layer_step, 0)

        total = lax.fori_loop(
            0,
            most,
            lambda f, total: total + jnp.sum(x[f].astype(F32), axis=0),
            jnp.zeros((ROWS, channels), F32),
        )
        mean = total / (jnp.broadcast_to(counts, (ROWS, channels)) * positions)
        pooled[pl.ds(first, ROWS), :] = mean.astype(BF16)
        return carry

    lax.fori_loop(0, blocks, block, 0)

    projected = jnp.dot(pooled[...], head_ref[...], preferred_element_type=F32)
    square = jnp.sum(projected * projected, axis=1, keepdims=True)
    vectors = (projected * lax.rsqrt(square + 1e-06)).astype(BF16)
    slots = lax.broadcasted_iota(jnp.int32, (clips, clips), 0)
    chosen = jnp.where(slots == place_ref[...], 1.0, 0.0).astype(BF16)
    out_ref[...] = jnp.dot(chosen, vectors, preferred_element_type=F32).astype(BF16)


def embed(clip_data, counts, places, expand_weight, depth_kernel, reduce_weight, head_weight):
    clips, frames, positions, channels = clip_data.shape
    layers, tap_count, expanded = depth_kernel.shape
    blocks = clips // ROWS
    slots = jnp.arange(clips, dtype=jnp.int32)
    ahead = (counts[None, :] > counts[:, None]) | (
        (counts[None, :] == counts[:, None]) & (slots[None, :] < slots[:, None])
    )
    rank = jnp.sum(ahead.astype(jnp.int32), axis=1)
    at_rank = rank[None, :] == slots[:, None]

    def ranked(values):
        return jnp.sum(jnp.where(at_rank, values[None, :], 0), axis=1)

    order, sorted_counts, sorted_places = ranked(slots), ranked(counts), ranked(places)
    vmem = pl.BlockSpec(memory_space=pltpu.VMEM)
    smem = pl.BlockSpec(memory_space=pltpu.SMEM)
    return pl.pallas_call(
        embed_kernel,
        out_shape=jax.ShapeDtypeStruct((clips, head_weight.shape[1]), BF16),
        in_specs=[smem, smem, pl.BlockSpec(memory_space=pl.ANY)] + [vmem] * 6,
        out_specs=vmem,
        scratch_shapes=[
            pltpu.VMEM((clips, frames, positions, channels), BF16),
            pltpu.VMEM((frames, positions, ROWS, channels), BF16),
            pltpu.VMEM((frames, positions, ROWS, expanded), BF16),
            pltpu.VMEM((positions, ROWS, expanded), BF16),
            pltpu.VMEM((clips, channels), BF16),
            pltpu.VMEM((layers, tap_count, ROWS, expanded), BF16),
            pltpu.SemaphoreType.DMA((blocks,)),
        ],
        compiler_params=pltpu.CompilerParams(vmem_limit_bytes=40 << 20),
        name="embed_clips",
    )(
        order,
        sorted_counts[::ROWS],
        clip_data,
        sorted_counts.astype(F32)[:, None],
        sorted_places[None, :],
        expand_weight,
        depth_kernel,
        reduce_weight,
        head_weight,
    )


def score_kernel(panel_size, known, part, rows_ref, label_ref, panel_ref, out_ref, best):
    step = pl.program_id(0)
    tile = panel_ref.shape[0]
    rows = rows_ref.shape[0]

    @pl.when(step == 0)
    def _():
        best[...] = jnp.full(best.shape, -jnp.inf, F32)

    for at in range(0, tile, part):
        scores = lax.dot_general(
            panel_ref[at : at + part, :],
            rows_ref[...],
            (((1,), (1,)), ((), ())),
            preferred_element_type=F32,
        )
        if at == 0:

            @pl.when(step == 0)
            def _():
                index = lax.broadcasted_iota(jnp.int32, (known, rows), 0)
                own = jnp.where(index == label_ref[...], scores[:known], -jnp.inf)
                out_ref[1:2, :] = jnp.max(own, axis=0, keepdims=True)

        place = step * tile + at + lax.broadcasted_iota(jnp.int32, scores.shape, 0)
        scores = jnp.where(place < panel_size, scores, -jnp.inf)
        best[...] = jnp.maximum(best[...], jnp.max(scores.reshape(part // 8, 8, rows), axis=0))

    @pl.when(step == pl.num_programs(0) - 1)
    def _():
        out_ref[0:1, :] = jnp.max(best[...], axis=0, keepdims=True)


def panel_scores(rows, labels, centroids, known):
    panel_size, width = centroids.shape
    count = rows.shape[0]
    tile, part = 1024, 256
    return pl.pallas_call(
        functools.partial(score_kernel, panel_size, known, part),
        out_shape=jax.ShapeDtypeStruct((2, count), F32),
        grid=(pl.cdiv(panel_size, tile),),
        in_specs=[
            pl.BlockSpec((count, width), lambda i: (0, 0)),
            pl.BlockSpec((1, count), lambda i: (0, 0)),
            pl.BlockSpec((tile, width), lambda i: (i, 0)),
        ],
        out_specs=pl.BlockSpec((2, count), lambda i: (0, 0)),
        scratch_shapes=[pltpu.VMEM((8, count), F32)],
        compiler_params=pltpu.CompilerParams(vmem_limit_bytes=40 << 20),
        name="panel_scores",
    )(rows, labels, centroids)


def local(
    clip_data,
    frame_counts,
    send_list,
    cluster_ids,
    expand_weight,
    depth_kernel,
    reduce_weight,
    head_weight,
    centroids,
):
    n_dp = lax.axis_size("dp")
    n_cent = lax.axis_size("cent")
    both = ("dp", "cent")
    clip_count = clip_data.shape[0]
    panel_size = centroids.shape[0]
    per_peer = clip_count // n_dp
    owner_total = n_dp * n_cent
    capacity = max(2, 4 * clip_count // owner_total)
    slot_total = owner_total * capacity
    me = lax.axis_index("dp") * n_cent + lax.axis_index("cent")

    def owner_of(ids):
        return ids % panel_size % n_dp * n_cent + ids // panel_size

    every_id = lax.all_gather(cluster_ids[0], both, axis=0)
    group_ids = lax.dynamic_slice_in_dim(
        every_id, lax.axis_index("dp") * n_cent, n_cent, axis=0
    ).reshape(1, n_cent * clip_count)
    labels = jnp.where(
        group_ids // panel_size == lax.axis_index("cent"), group_ids % panel_size, -1
    )
    mine = owner_of(every_id) == me
    slots = jnp.arange(clip_count, dtype=jnp.int32)
    before = (slots[:, None] < slots[None, :]).astype(BF16)
    rank_here = jnp.dot(mine.astype(BF16), before, preferred_element_type=F32).astype(jnp.int32)
    seats = jnp.arange(capacity, dtype=jnp.int32)
    seated = mine[:, None, :] & (rank_here[:, None, :] == seats[None, :, None])
    member_ids = (
        jnp.sum(jnp.where(seated, every_id[:, None, :] + 1, 0), axis=2).reshape(slot_total) - 1
    )

    given = cluster_ids[0]
    target = owner_of(given)
    earlier = (target[:, None] == target[None, :]) & (slots[None, :] < slots[:, None])
    seat = target * capacity + jnp.sum(earlier.astype(jnp.int32), axis=1)
    places = send_list[0] % n_dp * per_peer + send_list[0] // n_dp

    outgoing = embed(
        clip_data,
        frame_counts[0],
        places,
        expand_weight,
        depth_kernel,
        reduce_weight,
        head_weight,
    )
    width = outgoing.shape[1]
    vectors = (
        lax.all_to_all(
            outgoing.reshape(n_dp, per_peer, width), "dp", split_axis=0, concat_axis=0, tiled=True
        )
        .transpose(1, 0, 2)
        .reshape(clip_count, width)
    )
    block_rows = lax.all_gather(vectors, "cent", axis=0, tiled=True)

    at_seat = jnp.arange(slot_total, dtype=jnp.int32)[:, None] == seat[None, :]
    sent = jnp.dot(at_seat.astype(BF16), vectors, preferred_element_type=F32).astype(BF16)
    members = lax.all_to_all(
        sent.reshape(owner_total, capacity, width), both, split_axis=0, concat_axis=0, tiled=True
    ).reshape(slot_total, width)

    partial = panel_scores(block_rows, labels, centroids, GROUPS * n_dp)
    partial = partial.reshape(2, n_cent, clip_count).transpose(1, 0, 2)
    partial = lax.all_to_all(partial, "cent", split_axis=0, concat_axis=0, tiled=True)
    nearest, own_sim = jnp.max(partial, axis=0)

    similarity = jnp.einsum("rd,td->rt", members, members, preferred_element_type=F32)
    index = jnp.arange(slot_total, dtype=jnp.int32)
    same_cluster = (
        (member_ids[:, None] == member_ids[None, :])
        & (member_ids >= 0)[:, None]
        & (index[:, None] != index[None, :])
    )
    peer_values = jnp.max(jnp.where(same_cluster, similarity, -1.0), axis=1)
    back = lax.all_to_all(
        peer_values.reshape(owner_total, capacity), both, split_axis=0, concat_axis=0, tiled=True
    ).reshape(slot_total)
    peer_sim = jnp.max(jnp.where(at_seat, back[:, None], -1.0), axis=0)
    return (vectors, nearest, own_sim, peer_sim)


def solution(mesh):
    placed = (
        P(("dp", "cent"), None, None, None),
        P(("dp", "cent"), None),
        P(("dp", "cent"), None),
        P(("dp", "cent"), None),
        P(),
        P(),
        P(),
        P(),
        P("cent", None),
    )
    return jax.shard_map(
        local,
        mesh=mesh,
        in_specs=placed,
        out_specs=(
            P(("dp", "cent"), None),
            P(("dp", "cent")),
            P(("dp", "cent")),
            P(("dp", "cent")),
        ),
        check_vma=False,
    )
```

time: 508 us -> 217 us (0.43)
  other arithmetic: 253 us -> 6.04 us
  local copies, waits for them, and re-layouts: 123 us -> 14.3 us
  Pallas kernels: 0 us -> 81.7 us
  matrix products: 71 us -> 2.39 us
  blocking collectives: 7.05 us -> 55.3 us
  waiting for transfers between devices: 6.1 us -> 33 us
  starting transfers between devices: 27.5 us -> 9.46 us
    convert_element_type x65 -> x1, other arithmetic: 214 us -> 0.01 us  [embed(): sorted_counts.astype(F32)[:, None]]
    pallas_call x0 -> x2, Pallas kernels: none -> 81.7 us  [the longest x1 59.3 us: embed(): pl.pallas_call(embed_kernel, out_shape=jax.ShapeDtypeStruct((clips, head_...]
    dot_general x86 -> x3, matrix products: 71 us -> 2.39 us  [the longest x1 1.42 us: local(): jnp.dot(at_seat.astype(BF16), vectors, preferred_element_type=F32)]
    all_gather x0 -> x1, blocking collectives: none -> 39.3 us  [local(): every_id = lax.all_gather(cluster_ids[0], both, axis=0)]
    reshape x34 -> x0, local copies, waits for them, and re-layouts: 36.6 us -> none  [the longest x1 24.8 us: local(): panel_blocks = centroids.reshape(5, panel_size // 5, -1)]
    mul x64 -> x0, other arithmetic: 32.9 us -> none  [the longest x16 16.8 us: embed_clips(): features = clip_block * mask_four.astype(jnp.bfloat16)]
    scatter x4 -> x0, local copies, waits for them, and re-layouts: 27.7 us -> none  [the longest x1 18.6 us: local(): jnp.zeros((owner_total, capacity, width_d), jnp.bfloat16)]
    all_to_all x5 -> x3, waiting for transfers between devices: 5.59 us -> 32.9 us  [the longest x1 24 us: local(): lax.all_to_all(sent.reshape(owner_total, capacity, width), both, split_ax...]
  transfers between devices with their start and end apart: 6 -> 4, of which waited for: 1 -> 3; matrix products, arithmetic and copies ran while one was open for 20% -> 2% of each run, Pallas kernels for 0% -> 0%
where the time goes in v1:
time: 217 us; the launch traced here: 216 us
  Pallas kernels  81.7 us (38%)
  blocking collectives  55.3 us (25%)
  waiting for transfers between devices  33 us (15%)
  local copies, waits for them, and re-layouts  14.3 us (7%)
  between operations  14.3 us (7%)
  starting transfers between devices  9.46 us (4%)
  other arithmetic  6.04 us (3%)
  matrix products  2.39 us (1%)
    pallas_call x1, Pallas kernels, embed(): pl.pallas_call(embed_kernel, out_shape=jax.ShapeDtypeStruct((clips, head_...  59.3 us
    all_gather x1, blocking collectives, local(): every_id = lax.all_gather(cluster_ids[0], both, axis=0)  39.3 us
    all_to_all x1, waiting for transfers between devices, local(): lax.all_to_all(sent.reshape(owner_total, capacity, width), both, split_ax...  24 us
    pallas_call x1, Pallas kernels, panel_scores(): pl.pallas_call(functools.partial(score_kernel, panel_size, known, part),...  22.4 us
    all_to_all x1, blocking collectives, local(): lax.all_to_all(outgoing.reshape(n_dp, per_peer, width), 'dp', split_axis=...  16 us
    unnamed x19, local copies, waits for them, and re-layouts  11.4 us
    all_to_all x1, waiting for transfers between devices, local(): lax.all_to_all(peer_values.reshape(owner_total, capacity), both, split_ax...  6.63 us
  transfers between devices with their start and end apart: 4, of which 3 were waited for; matrix products, arithmetic and copies ran while one was open for 2% of the time, Pallas kernels for 0%

profile of v1, /device:TPU:0, one launch (start us, length us, event | category | flops | bytes accessed | tf_op | source)
XLA Modules:
  0.0 216.4 jit_solution(12142130243417298365)
XLA Ops:
  7.3 0.8 fusion.25
  8.0 0.9 convert_reduce_fusion.1
  8.9 0.8 select_reduce_fusion.2
  9.8 7.8 %copy.42.clip_ref = bf16[128,4,16,192]{3,2,1,0:T(8,128)(2,1)} copy(bf16[128,4,16,192]{0,3,2,1:T(8,128)(2,1)} %param.9) | data formatting | bytes 6291456 | tf_op args[0]
  18.0 2.2 %copy-done = bf16[128,4,16,192]{3,2,1,0:T(8,128)(2,1)S(1)} copy-done((bf16[128,4,16,192]{3,2,1,0:T(8,128)(2,1)S(1)}, bf16[128,4,16,192]{3,2,1,0:T(8,128)(2,1)}, u32[]{:S(2)}) %copy-start) | copy-done | bytes 3145752
  20.2 59.3 %embed_clips.1 = bf16[128,1024]{1,0:T(8,128)(2,1)S(1)} custom-call(s32[128]{0:T(128)S(1)} %get-tuple-element.6.order_ref, s32[8]{0:T(128)S(1)} %slice.3.most_ref, bf16[128,4,16,192]{3,2,1,0:T(8,128)(2,1)S(1)} %copy-done, f32[128,1]{1,0:T(8,128)S(1)} %copy.43.count_ref, s32[1,128]{1,0:T(1,128)S(1)} %bitcast.83, bf16[2,192,432]{2,1,0:T(8,128)(2,1)S(1)} %copy-done.2, ...), custom_call_target="tpu_custom_call" | custom-call | tf_op jit(solution)/shard_map/embed_clips/pallas_call | solution.py:171
  79.4 16.0 %all_to_all.24 = bf16[8,16,1024]{2,1,0:T(8,128)(2,1)S(1)} all-to-all(bf16[8,16,1024]{2,1,0:T(8,128)(2,1)S(1)} %bitcast.82), channel_id=1, replica_groups=mesh['dp'=8,'cent'=4] {'dp'}, dimensions={0} | all-to-all | bytes 524288 | tf_op jit(solution)/shard_map/all_to_all | solution.py:312
  95.4 0.9 copy.54
  96.3 39.3 %all-gather = s32[32,1,128]{2,1,0:T(1,128)S(1)} all-gather(s32[1,1,128]{2,1,0:T(1,128)S(1)} %bitcast.93), channel_id=1, replica_groups=mesh['dp'=8,'cent'=4] {'dp','cent'}, dimensions={0}, use_global_device_ids=true | all-gather | bytes 16896 | tf_op jit(solution)/shard_map/all_gather | solution.py:278
  135.9 1.2 copy-done.1
  137.2 22.4 %panel_scores.1 = f32[2,512]{1,0:T(2,128)} custom-call(bf16[512,1024]{1,0:T(8,128)(2,1)S(1)} %copy-done.1, s32[1,512]{1,0:T(1,128)S(1)} %compare_select_fusion.label_ref, bf16[12500,1024]{1,0:T(8,128)(2,1)} %panel_ref.1), custom_call_target="tpu_custom_call" | custom-call | tf_op jit(solution)/shard_map/panel_scores/pallas_call | solution.py:237
  159.6 3.2 %all-to-all-start.1 = ((f32[4,2,128]{2,1,0:T(2,128)}), f32[4,2,128]{2,1,0:T(2,128)S(1)}, u32[]{:S(2)}, u32[]{:S(2)}) async-start(f32[4,2,128]{2,1,0:T(2,128)} %bitcast.12), calls=%async_computation.1 | async-start | bytes 8192 | tf_op jit(solution)/shard_map/all_to_all | solution.py:328
  162.8 1.4 convolution_convert_fusion
  164.2 2.3 %all-to-all-done.1 = f32[4,2,128]{2,1,0:T(2,128)S(1)} async-done(((f32[4,2,128]{2,1,0:T(2,128)}), f32[4,2,128]{2,1,0:T(2,128)S(1)}, u32[]{:S(2)}, u32[]{:S(2)}) %all-to-all-start.1) | async-done | bytes 4128 | tf_op jit(solution)/shard_map/all_to_all | solution.py:328
  166.6 2.6 %all-to-all-start.2 = ((bf16[32,16,1024]{2,1,0:T(8,128)(2,1)}), bf16[32,16,1024]{2,1,0:T(8,128)(2,1)S(1)}, u32[]{:S(2)}, u32[]{:S(2)}) async-start(bf16[32,16,1024]{2,1,0:T(8,128)(2,1)} %bitcast.29), calls=%async_computation.2 | async-start | bytes 2097152 | tf_op jit(solution)/shard_map/all_to_all | solution.py:322
  169.2 1.3 div.58
  170.7 0.6 select_reduce_fusion.1
  171.4 24.0 %all-to-all-done.2 = bf16[32,16,1024]{2,1,0:T(8,128)(2,1)S(1)} async-done(((bf16[32,16,1024]{2,1,0:T(8,128)(2,1)}), bf16[32,16,1024]{2,1,0:T(8,128)(2,1)S(1)}, u32[]{:S(2)}, u32[]{:S(2)}) %all-to-all-start.2) | async-done | bytes 1048608 | tf_op jit(solution)/shard_map/all_to_all | solution.py:322
  195.4 0.8 fusion
  196.3 0.7 all_to_all.18
  196.9 3.5 %all-to-all-start.3 = ((f32[32,1,16]{2,1,0:T(1,128)}), f32[32,1,16]{2,1,0:T(1,128)S(1)}, u32[]{:S(2)}, u32[]{:S(2)}) async-start(f32[32,1,16]{2,1,0:T(1,128)} %bitcast.31), calls=%async_computation.3 | async-start | bytes 32768 | tf_op jit(solution)/shard_map/all_to_all | solution.py:339
  201.0 6.6 %all-to-all-done.3 = f32[32,1,16]{2,1,0:T(1,128)S(1)} async-done(((f32[32,1,16]{2,1,0:T(1,128)}), f32[32,1,16]{2,1,0:T(1,128)S(1)}, u32[]{:S(2)}, u32[]{:S(2)}) %all-to-all-start.3) | async-done | bytes 2080 | tf_op jit(solution)/shard_map/all_to_all | solution.py:339
  208.2 0.7 reduce.3
  208.9 0.7 select_reduce_fusion
  (38 shorter events, 2.2 us)
Async XLA Ops:
  7.2 10.5 %copy-start.6 = (bf16[2,27,432]{2,0,1:T(2,128)(2,1)S(1)}, bf16[2,27,432]{2,0,1:T(2,128)(2,1)}, u32[]{:S(2)}) copy-start(bf16[2,27,432]{2,0,1:T(2,128)(2,1)} %param.14) | copy-start | bytes 139972
  7.2 10.6 %copy-start.5 = (bf16[2,432,192]{1,2,0:T(8,128)(2,1)S(1)}, bf16[2,432,192]{1,2,0:T(8,128)(2,1)}, u32[]{:S(2)}) copy-start(bf16[2,432,192]{1,2,0:T(8,128)(2,1)} %param.15) | copy-start | bytes 995332
  7.2 10.8 %copy-start.2 = (bf16[2,192,432]{2,1,0:T(8,128)(2,1)S(1)}, bf16[2,192,432]{2,1,0:T(8,128)(2,1)}, u32[]{:S(2)}) copy-start(bf16[2,192,432]{2,1,0:T(8,128)(2,1)} %expand_ref.1) | copy-start | bytes 995332
  7.2 10.8 %copy-start.3 = (bf16[192,1024]{1,0:T(8,128)(2,1)S(1)}, bf16[192,1024]{1,0:T(8,128)(2,1)}, u32[]{:S(2)}) copy-start(bf16[192,1024]{1,0:T(8,128)(2,1)} %head_ref.1) | copy-start | bytes 1179652
  7.2 128.7 %all-gather.3.cloned.1.call-start = ((), (), s32[]{:S(2)}) async-start(), calls=%async_computation.4 | async-start | bytes 1310720 | tf_op jit(solution)/shard_map/all_gather | solution.py:318
  17.6 78.7 %copy-start.7 = (s32[1,128]{1,0:T(1,128)S(1)}, s32[1,128]{1,0:T(1,128)}, u32[]{:S(2)}) copy-start(s32[1,128]{1,0:T(1,128)} %param.12) | copy-start | bytes 1540
  18.0 2.2 %copy-start = (bf16[128,4,16,192]{3,2,1,0:T(8,128)(2,1)S(1)}, bf16[128,4,16,192]{3,2,1,0:T(8,128)(2,1)}, u32[]{:S(2)}) copy-start(bf16[128,4,16,192]{3,2,1,0:T(8,128)(2,1)} %copy.42.clip_ref) | copy-start | bytes 9437188
  135.9 1.2 copy-start.1
  137.2 25.6 %copy-start.4 = (bf16[16,8,1024]{2,1,0:T(8,128)(2,1)S(1)}, bf16[16,8,1024]{2,1,0:T(8,128)(2,1)}, u32[]{:S(2)}) copy-start(bf16[16,8,1024]{2,1,0:T(8,128)(2,1)} %copy.54) | copy-start | bytes 786436
  159.6 7.0 %all-to-all-start.1 = ((f32[4,2,128]{2,1,0:T(2,128)}), f32[4,2,128]{2,1,0:T(2,128)S(1)}, u32[]{:S(2)}, u32[]{:S(2)}) async-start(f32[4,2,128]{2,1,0:T(2,128)} %bitcast.12), calls=%async_computation.1 | async-start | bytes 8192 | tf_op jit(solution)/shard_map/all_to_all | solution.py:328
  166.6 28.9 %all-to-all-start.2 = ((bf16[32,16,1024]{2,1,0:T(8,128)(2,1)}), bf16[32,16,1024]{2,1,0:T(8,128)(2,1)S(1)}, u32[]{:S(2)}, u32[]{:S(2)}) async-start(bf16[32,16,1024]{2,1,0:T(8,128)(2,1)} %bitcast.29), calls=%async_computation.2 | async-start | bytes 2097152 | tf_op jit(solution)/shard_map/all_to_all | solution.py:322
  196.9 10.7 %all-to-all-start.3 = ((f32[32,1,16]{2,1,0:T(1,128)}), f32[32,1,16]{2,1,0:T(1,128)S(1)}, u32[]{:S(2)}, u32[]{:S(2)}) async-start(f32[32,1,16]{2,1,0:T(1,128)} %bitcast.31), calls=%async_computation.3 | async-start | bytes 32768 | tf_op jit(solution)/shard_map/all_to_all | solution.py:339
Sparse Core Ops, SparseCore 0:
  96.4 15.7 all-gather.2

commit v2 on v1

--- a/solution.py
+++ b/solution.py
@@ -15,8 +15,8 @@
 
 
 def embed_kernel(
+    most_ref,
     order_ref,
-    most_ref,
     clip_ref,
     count_ref,
     place_ref,
@@ -25,37 +25,41 @@
     reduce_ref,
     head_ref,
     out_ref,
-    arrived,
     x,
     hidden,
     activated,
     pooled,
     taps,
-    sems,
 ):
-    clips, frames, positions, channels = clip_ref.shape
+    frames, positions, channels, clips = clip_ref.shape
     layers, tap_count, expanded = depth_ref.shape
     blocks = clips // ROWS
     flat = positions * ROWS
 
-    def fetch(i, carry):
-        pltpu.make_async_copy(
-            clip_ref.at[order_ref[i]], arrived.at[i], sems.at[i // ROWS]
-        ).start()
+    clip_of = lax.broadcasted_iota(jnp.int32, (clips, clips), 1)
+    by_count = jnp.where(clip_of == order_ref[...], 1.0, 0.0).astype(BF16)
+    every_count = jnp.broadcast_to(count_ref[...], (clips, channels))
+
+    def load(f, carry):
+        kept = jnp.where(every_count > f.astype(F32), 1.0, 0.0)
+
+        def place(p, carry):
+            ranked = lax.dot_general(
+                by_count, clip_ref[f, p], (((1,), (1,)), ((), ())), preferred_element_type=F32
+            )
+            x[f, p] = (ranked * kept).astype(BF16)
+            return carry
+
+        lax.fori_loop(0, positions, place, 0, unroll=4)
         return carry
 
-    lax.fori_loop(0, clips, fetch, 0)
+    lax.fori_loop(0, most_ref[0], load, 0)
 
     for layer in range(layers):
         rows = depth_ref[layer].astype(F32)
         for t in range(tap_count):
             taps[layer, t] = jnp.broadcast_to(rows[t : t + 1], (ROWS, expanded)).astype(BF16)
 
-    to_row = lax.broadcasted_iota(jnp.int32, (flat, flat), 0)
-    from_row = lax.broadcasted_iota(jnp.int32, (flat, flat), 1)
-    turn = jnp.where(
-        from_row == (to_row % ROWS) * positions + to_row // ROWS, 1.0, 0.0
-    ).astype(BF16)
     lanes = [(at, min(at + 128, expanded)) for at in range(0, expanded, 128)]
 
     def convolve(layer, f, shifts):
@@ -83,27 +87,16 @@
     def block(b, carry):
         most = most_ref[b]
         first = pl.multiple_of(b * ROWS, ROWS)
-        pltpu.make_async_copy(
-            clip_ref.at[pl.ds(0, ROWS)], arrived.at[pl.ds(first, ROWS)], sems.at[b]
-        ).wait()
         counts = count_ref[pl.ds(first, ROWS), :]
 
         def mask(f, width):
             wide = jnp.broadcast_to(counts, (ROWS, width))
             return jnp.where(wide > f.astype(F32), 1.0, 0.0)
 
-        def load(f, carry):
-            raw = arrived[pl.ds(first, ROWS), f].reshape(flat, channels)
-            turned = jnp.dot(turn, raw, preferred_element_type=F32)
-            x[f] = (turned.reshape(positions, ROWS, channels) * mask(f, channels)[None]).astype(BF16)
-            return carry
-
-        lax.fori_loop(0, most, load, 0)
-
         def layer_step(layer, carry):
             def expand(f, carry):
                 wide = jnp.dot(
-                    x[f].reshape(flat, channels), expand_ref[layer], preferred_element_type=F32
+                    x[f, :, pl.ds(first, ROWS), :].reshape(flat, channels), expand_ref[layer], preferred_element_type=F32
                 )
                 wide = jnp.maximum(wide, 0.0).astype(BF16).reshape(positions, ROWS, expanded)
                 hidden[f] = wide * mask(f, expanded).astype(BF16)[None]
@@ -123,7 +116,10 @@
                     reduce_ref[layer],
                     preferred_element_type=F32,
                 ).reshape(positions, ROWS, channels)
-                x[f] = (x[f].astype(F32) + branch * mask(f, channels)[None]).astype(BF16)
+                kept = x[f, :, pl.ds(first, ROWS), :].astype(F32)
+                x[f, :, pl.ds(first, ROWS), :] = (
+                    kept + branch * mask(f, channels)[None]
+                ).astype(BF16)
                 return carry
 
             lax.fori_loop(0, most, mix, 0)
@@ -134,7 +130,7 @@
         total = lax.fori_loop(
             0,
             most,
-            lambda f, total: total + jnp.sum(x[f].astype(F32), axis=0),
+            lambda f, total: total + jnp.sum(x[f, :, pl.ds(first, ROWS), :].astype(F32), axis=0),
             jnp.zeros((ROWS, channels), F32),
         )
         mean = total / (jnp.broadcast_to(counts, (ROWS, channels)) * positions)
@@ -154,7 +150,6 @@
 def embed(clip_data, counts, places, expand_weight, depth_kernel, reduce_weight, head_weight):
     clips, frames, positions, channels = clip_data.shape
     layers, tap_count, expanded = depth_kernel.shape
-    blocks = clips // ROWS
     slots = jnp.arange(clips, dtype=jnp.int32)
     ahead = (counts[None, :] > counts[:, None]) | (
         (counts[None, :] == counts[:, None]) & (slots[None, :] < slots[:, None])
@@ -171,23 +166,21 @@
     return pl.pallas_call(
         embed_kernel,
         out_shape=jax.ShapeDtypeStruct((clips, head_weight.shape[1]), BF16),
-        in_specs=[smem, smem, pl.BlockSpec(memory_space=pl.ANY)] + [vmem] * 6,
+        in_specs=[smem] + [vmem] * 8,
         out_specs=vmem,
         scratch_shapes=[
-            pltpu.VMEM((clips, frames, positions, channels), BF16),
-            pltpu.VMEM((frames, positions, ROWS, channels), BF16),
+            pltpu.VMEM((frames, positions, clips, channels), BF16),
             pltpu.VMEM((frames, positions, ROWS, expanded), BF16),
             pltpu.VMEM((positions, ROWS, expanded), BF16),
             pltpu.VMEM((clips, channels), BF16),
             pltpu.VMEM((layers, tap_count, ROWS, expanded), BF16),
-            pltpu.SemaphoreType.DMA((blocks,)),
         ],
         compiler_params=pltpu.CompilerParams(vmem_limit_bytes=40 << 20),
         name="embed_clips",
     )(
-        order,
         sorted_counts[::ROWS],
-        clip_data,
+        order[:, None],
+        clip_data.transpose(1, 2, 3, 0),
         sorted_counts.astype(F32)[:, None],
         sorted_places[None, :],
         expand_weight,
@@ -198,7 +191,7 @@
 
 
 def score_kernel(panel_size, known, part, rows_ref, label_ref, panel_ref, out_ref, best):
-    step = pl.program_id(0)
+    step, final = pl.program_id(0), pl.num_programs(0) - 1
     tile = panel_ref.shape[0]
     rows = rows_ref.shape[0]
 
@@ -221,9 +214,17 @@
                 own = jnp.where(index == label_ref[...], scores[:known], -jnp.inf)
                 out_ref[1:2, :] = jnp.max(own, axis=0, keepdims=True)
 
-        place = step * tile + at + lax.broadcasted_iota(jnp.int32, scores.shape, 0)
-        scores = jnp.where(place < panel_size, scores, -jnp.inf)
-        best[...] = jnp.maximum(best[...], jnp.max(scores.reshape(part // 8, 8, rows), axis=0))
+        def keep(values):
+            best[...] = jnp.maximum(best[...], jnp.max(values.reshape(part // 8, 8, rows), axis=0))
+
+        @pl.when(step < final)
+        def _():
+            keep(scores)
+
+        @pl.when(step == final)
+        def _():
+            place = step * tile + at + lax.broadcasted_iota(jnp.int32, scores.shape, 0)
+            keep(jnp.where(place < panel_size, scores, -jnp.inf))
 
     @pl.when(step == pl.num_programs(0) - 1)
     def _():
@@ -250,6 +251,147 @@
     )(rows, labels, centroids)
 
 
+def exchange_kernel(
+    n_dp,
+    n_cent,
+    outgoing_ref,
+    seat_ref,
+    vectors_ref,
+    rows_ref,
+    members_ref,
+    landed,
+    rows,
+    leaving,
+    members,
+    shuffle_send,
+    shuffle_recv,
+    gather_send,
+    gather_recv,
+    member_send,
+    member_recv,
+):
+    dp, cent = lax.axis_index("dp"), lax.axis_index("cent")
+    per_peer, width = outgoing_ref.shape[1:]
+    clips = n_dp * per_peer
+    seats = members.shape[2]
+    mesh_id = pl.DeviceIdType.MESH
+    chips = n_cent // 2
+    chip, core = cent // 2, cent % 2
+
+    barrier = pltpu.get_barrier_semaphore()
+    for s in range(1, n_dp):
+        pl.semaphore_signal(
+            barrier, inc=1, device_id=((dp + s) % n_dp, cent), device_id_type=mesh_id
+        )
+    for s in range(1, n_cent):
+        pl.semaphore_signal(
+            barrier, inc=1, device_id=(dp, (cent + s) % n_cent), device_id_type=mesh_id
+        )
+    pl.semaphore_wait(barrier, n_dp + n_cent - 2)
+
+    shuffles = []
+    for s in range(1, n_dp):
+        peer = (dp + s) % n_dp
+        copy = pltpu.make_async_remote_copy(
+            src_ref=outgoing_ref.at[peer],
+            dst_ref=landed.at[dp],
+            send_sem=shuffle_send.at[s],
+            recv_sem=shuffle_recv.at[s],
+            device_id=(peer, cent),
+            device_id_type=mesh_id,
+        )
+        copy.start()
+        shuffles.append(copy)
+    landed[dp] = outgoing_ref[dp]
+    for copy in shuffles:
+        copy.wait()
+
+    to_row = lax.broadcasted_iota(jnp.int32, (clips, clips), 0)
+    from_row = lax.broadcasted_iota(jnp.int32, (clips, clips), 1)
+    turn = jnp.where(from_row == to_row % n_dp * per_peer + to_row // n_dp, 1.0, 0.0)
+    vectors = jnp.dot(
+        turn.astype(BF16), landed[...].reshape(clips, width), preferred_element_type=F32
+    ).astype(BF16)
+    vectors_ref[...] = vectors
+    rows[cent] = vectors
+
+    gathers, sources = [None], [cent]
+    for i in range(1, n_cent):
+        hop, side = i // 2, i % 2
+        sources.append((chip + hop) % chips * 2 + (core + side) % 2)
+        copy = pltpu.make_async_remote_copy(
+            src_ref=rows.at[cent],
+            dst_ref=rows.at[cent],
+            send_sem=gather_send.at[i],
+            recv_sem=gather_recv.at[i],
+            device_id=(dp, (chip + chips - hop) % chips * 2 + (core + side) % 2),
+            device_id_type=mesh_id,
+        )
+        copy.start()
+        gathers.append(copy)
+
+    seat_of = lax.broadcasted_iota(jnp.int32, (n_dp * seats, clips), 0)
+    handed = []
+    for i, source in enumerate(sources):
+        if i:
+            gathers[i].wait_recv()
+        chosen = jnp.where(seat_of == seat_ref[source], 1.0, 0.0).astype(BF16)
+        seated = jnp.dot(chosen, rows[source], preferred_element_type=F32).astype(BF16)
+        leaving[i] = seated.reshape(n_dp, seats, width)
+        for s in range(1, n_dp):
+            peer = (dp + s) % n_dp
+            copy = pltpu.make_async_remote_copy(
+                src_ref=leaving.at[i, peer],
+                dst_ref=members.at[dp, source],
+                send_sem=member_send.at[i, s],
+                recv_sem=member_recv.at[i, s],
+                device_id=(peer, cent),
+                device_id_type=mesh_id,
+            )
+            copy.start()
+            handed.append(copy)
+        members[dp, source] = leaving[i, dp]
+    for copy in gathers[1:]:
+        copy.wait_send()
+    rows_ref[...] = rows[...]
+    for copy in handed:
+        copy.wait()
+    members_ref[...] = members[...]
+
+
+def exchange(outgoing, seat_of_row, n_dp, n_cent, seats):
+    per_peer, width = outgoing.shape[1:]
+    clips = n_dp * per_peer
+    vmem = pl.BlockSpec(memory_space=pltpu.VMEM)
+    dma = pltpu.SemaphoreType.DMA
+    return pl.pallas_call(
+        functools.partial(exchange_kernel, n_dp, n_cent),
+        out_shape=(
+            jax.ShapeDtypeStruct((clips, width), BF16),
+            jax.ShapeDtypeStruct((n_cent, clips, width), BF16),
+            jax.ShapeDtypeStruct((n_dp, n_cent, seats, width), BF16),
+        ),
+        in_specs=[vmem] * 2,
+        out_specs=(vmem,) * 3,
+        scratch_shapes=[
+            pltpu.VMEM((n_dp, per_peer, width), BF16),
+            pltpu.VMEM((n_cent, clips, width), BF16),
+            pltpu.VMEM((n_cent, n_dp, seats, width), BF16),
+            pltpu.VMEM((n_dp, n_cent, seats, width), BF16),
+            dma((n_dp,)),
+            dma((n_dp,)),
+            dma((n_cent,)),
+            dma((n_cent,)),
+            dma((n_cent, n_dp)),
+            dma((n_cent, n_dp)),
+        ],
+        compiler_params=pltpu.CompilerParams(
+            collective_id=0, has_side_effects=True, vmem_limit_bytes=40 << 20
+        ),
+        name="exchange",
+    )(outgoing, seat_of_row)
+
+
 def local(
     clip_data,
     frame_counts,
@@ -268,7 +410,7 @@
     panel_size = centroids.shape[0]
     per_peer = clip_count // n_dp
     owner_total = n_dp * n_cent
-    capacity = max(2, 4 * clip_count // owner_total)
+    capacity = max(ROWS, 4 * clip_count // owner_total)
     slot_total = owner_total * capacity
     me = lax.axis_index("dp") * n_cent + lax.axis_index("cent")
 
@@ -278,10 +420,9 @@
     every_id = lax.all_gather(cluster_ids[0], both, axis=0)
     group_ids = lax.dynamic_slice_in_dim(
         every_id, lax.axis_index("dp") * n_cent, n_cent, axis=0
-    ).reshape(1, n_cent * clip_count)
-    labels = jnp.where(
-        group_ids // panel_size == lax.axis_index("cent"), group_ids % panel_size, -1
-    )
+    ).reshape(n_cent, clip_count)
+    here = group_ids // panel_size == lax.axis_index("cent")
+    labels = jnp.where(here, group_ids % panel_size, -1).reshape(1, n_cent * clip_count)
     mine = owner_of(every_id) == me
     slots = jnp.arange(clip_count, dtype=jnp.int32)
     before = (slots[:, None] < slots[None, :]).astype(BF16)
@@ -292,10 +433,10 @@
         jnp.sum(jnp.where(seated, every_id[:, None, :] + 1, 0), axis=2).reshape(slot_total) - 1
     )
 
-    given = cluster_ids[0]
-    target = owner_of(given)
-    earlier = (target[:, None] == target[None, :]) & (slots[None, :] < slots[:, None])
+    target = jnp.where(here, group_ids % panel_size % n_dp, -1)
+    earlier = (target[:, :, None] == target[:, None, :]) & (slots[:, None] < slots[None, :])
     seat = target * capacity + jnp.sum(earlier.astype(jnp.int32), axis=1)
+    seat = jnp.where(here, seat, -1)
     places = send_list[0] % n_dp * per_peer + send_list[0] // n_dp
 
     outgoing = embed(
@@ -308,26 +449,11 @@
         head_weight,
     )
     width = outgoing.shape[1]
-    vectors = (
-        lax.all_to_all(
-            outgoing.reshape(n_dp, per_peer, width), "dp", split_axis=0, concat_axis=0, tiled=True
-        )
-        .transpose(1, 0, 2)
-        .reshape(clip_count, width)
-    )
-    block_rows = lax.all_gather(vectors, "cent", axis=0, tiled=True)
-
-    at_seat = jnp.arange(slot_total, dtype=jnp.int32)[:, None] == seat[None, :]
-    sent = jnp.dot(at_seat.astype(BF16), vectors, preferred_element_type=F32).astype(BF16)
-    members = lax.all_to_all(
-        sent.reshape(owner_total, capacity, width), both, split_axis=0, concat_axis=0, tiled=True
-    ).reshape(slot_total, width)
-
-    partial = panel_scores(block_rows, labels, centroids, GROUPS * n_dp)
-    partial = partial.reshape(2, n_cent, clip_count).transpose(1, 0, 2)
-    partial = lax.all_to_all(partial, "cent", split_axis=0, concat_axis=0, tiled=True)
-    nearest, own_sim = jnp.max(partial, axis=0)
-
+    vectors, block_rows, members = exchange(
+        outgoing.reshape(n_dp, per_peer, width), seat[:, None, :], n_dp, n_cent, capacity
+    )
+    block_rows = block_rows.reshape(n_cent * clip_count, width)
+    members = members.reshape(slot_total, width)
     similarity = jnp.einsum("rd,td->rt", members, members, preferred_element_type=F32)
     index = jnp.arange(slot_total, dtype=jnp.int32)
     same_cluster = (
@@ -337,9 +463,21 @@
     )
     peer_values = jnp.max(jnp.where(same_cluster, similarity, -1.0), axis=1)
     back = lax.all_to_all(
-        peer_values.reshape(owner_total, capacity), both, split_axis=0, concat_axis=0, tiled=True
-    ).reshape(slot_total)
-    peer_sim = jnp.max(jnp.where(at_seat, back[:, None], -1.0), axis=0)
+        peer_values.reshape(n_dp, n_cent, capacity),
+        "dp",
+        split_axis=0,
+        concat_axis=0,
+        tiled=True,
+    )
+    back = back.transpose(1, 0, 2).reshape(n_cent, n_dp * capacity)
+    at_seat = jnp.arange(n_dp * capacity, dtype=jnp.int32)[None, :, None] == seat[:, None, :]
+    peers = jnp.max(jnp.where(at_seat, back[:, :, None], -1.0), axis=1)
+    scored = panel_scores(block_rows, labels, centroids, GROUPS * n_dp)
+    partial = jnp.concatenate([scored.reshape(2, n_cent, clip_count), peers[None]], axis=0)
+    partial = lax.all_to_all(
+        partial.transpose(1, 0, 2), "cent", split_axis=0, concat_axis=0, tiled=True
+    )
+    nearest, own_sim, peer_sim = jnp.max(partial, axis=0)
     return (vectors, nearest, own_sim, peer_sim)
 
 

time: 217 us -> 184 us (0.85)
  Pallas kernels: 81.7 us -> 114 us
  waiting for transfers between devices: 33 us -> 3.78 us
  between operations: 14.3 us -> 0.78 us
  blocking collectives: 55.3 us -> 43.2 us
  local copies, waits for them, and re-layouts: 14.3 us -> 8.31 us
    pallas_call x0 -> x1, Pallas kernels: none -> 33.5 us  [exchange(): pl.pallas_call(functools.partial(exchange_kernel, n_dp, n_cent), out_shap...]
    all_to_all x3 -> x2, waiting for transfers between devices: 32.9 us -> 3.78 us  [the longest x1 3.78 us: local(): lax.all_to_all(partial.transpose(1, 0, 2), 'cent', split_axis=0, concat_a...]
    all_to_all x1 -> x0, blocking collectives: 16 us -> none  [local(): lax.all_to_all(outgoing.reshape(n_dp, per_peer, width), 'dp', split_axis=...]
    pallas_call x1, Pallas kernels: 59.3 us -> 52.9 us  [embed(): pl.pallas_call(embed_kernel, out_shape=jax.ShapeDtypeStruct((clips, head_...]
    pallas_call x1, Pallas kernels: 22.4 us -> 27.8 us  [panel_scores(): pl.pallas_call(functools.partial(score_kernel, panel_size, known, part),...]
    unnamed x19 -> x9, local copies, waits for them, and re-layouts: 11.4 us -> 6.6 us
    all_gather x1, blocking collectives: 39.3 us -> 43.2 us  [local(): every_id = lax.all_gather(cluster_ids[0], both, axis=0)]
    all_to_all x3 -> x2, starting transfers between devices: 9.42 us -> 7.32 us  [the longest x1 4.07 us: local(): lax.all_to_all(peer_values.reshape(n_dp, n_cent, capacity), 'dp', split_a...]
  transfers between devices with their start and end apart: 4 -> 2, of which waited for: 3 -> 1; matrix products, arithmetic and copies ran while one was open for 2% -> 0% of each run, Pallas kernels for 0% -> 15%
where the time goes in v2:
time: 184 us
  Pallas kernels  114 us (62%)
  blocking collectives  43.2 us (23%)
  local copies, waits for them, and re-layouts  8.31 us (5%)
  starting transfers between devices  7.32 us (4%)
  other arithmetic  5.34 us (3%)
  waiting for transfers between devices  3.78 us (2%)
    pallas_call x1, Pallas kernels, embed(): pl.pallas_call(embed_kernel, out_shape=jax.ShapeDtypeStruct((clips, head_...  52.9 us
    all_gather x1, blocking collectives, local(): every_id = lax.all_gather(cluster_ids[0], both, axis=0)  43.2 us
    pallas_call x1, Pallas kernels, exchange(): pl.pallas_call(functools.partial(exchange_kernel, n_dp, n_cent), out_shap...  33.5 us
    pallas_call x1, Pallas kernels, panel_scores(): pl.pallas_call(functools.partial(score_kernel, panel_size, known, part),...  27.8 us
    unnamed x9, local copies, waits for them, and re-layouts  6.6 us
    all_to_all x1, starting transfers between devices, local(): lax.all_to_all(peer_values.reshape(n_dp, n_cent, capacity), 'dp', split_a...  4.07 us
    all_to_all x1, waiting for transfers between devices, local(): lax.all_to_all(partial.transpose(1, 0, 2), 'cent', split_axis=0, concat_a...  3.78 us
  transfers between devices with their start and end apart: 2, of which 1 were waited for; matrix products, arithmetic and copies ran while one was open for 0% of the time, Pallas kernels for 15%

profile of v2, /device:TPU:0, one launch (start us, length us, event | category | flops | bytes accessed | tf_op | source)
XLA Modules:
  0.0 184.0 jit_solution(1582638801385812126)
XLA Ops:
  0.6 0.9 convert_reduce_fusion.1
  1.5 0.7 fusion.20
  2.2 0.8 select_reduce_fusion.2
  3.2 43.2 %all-gather = s32[32,1,128]{2,1,0:T(1,128)S(1)} all-gather(s32[1,1,128]{2,1,0:T(1,128)} %bitcast.100), channel_id=1, replica_groups=mesh['dp'=8,'cent'=4] {'dp','cent'}, dimensions={0}, use_global_device_ids=true | all-gather | bytes 16896 | tf_op jit(solution)/shard_map/all_gather | solution.py:420
  46.4 1.3 div.31
  47.9 0.6 select_reduce_fusion.1
  48.6 0.2 convert_reduce_fusion
  49.0 0.8 copy.42.depth_ref
  49.8 1.2 copy.43.reduce_ref
  51.1 1.9 %copy-done = bf16[128,4,16,192]{0,3,2,1:T(8,128)(2,1)S(1)} copy-done((bf16[128,4,16,192]{0,3,2,1:T(8,128)(2,1)S(1)}, bf16[128,4,16,192]{0,3,2,1:T(8,128)(2,1)}, u32[]{:S(2)}) %copy-start) | copy-done | bytes 3145752
  52.9 1.0 copy-done.1
  53.9 1.0 copy-done.2
  54.9 52.9 %embed_clips.1 = bf16[128,1024]{1,0:T(8,128)(2,1)S(1)} custom-call(s32[8]{0:T(128)S(1)} %slice.3.most_ref, s32[128,1]{1,0:T(8,128)S(1)} %copy.40.order_ref, bf16[4,16,192,128]{3,2,1,0:T(8,128)(2,1)S(1)} %bitcast.83, f32[128,1]{1,0:T(8,128)S(1)} %copy.41.count_ref, s32[1,128]{1,0:T(1,128)S(1)} %bitcast.89, bf16[2,192,432]{2,1,0:T(8,128)(2,1)S(1)} %copy-done.1, ...), custom_call_target="tpu_custom_call" | custom-call | tf_op jit(solution)/shard_map/embed_clips/pallas_call | solution.py:166
  107.9 33.5 %exchange.1 = (bf16[128,1024]{1,0:T(8,128)(2,1)S(1)}, bf16[4,128,1024]{2,1,0:T(8,128)(2,1)S(1)}, bf16[8,4,16,1024]{3,2,1,0:T(8,128)(2,1)S(1)}) custom-call(bf16[8,16,1024]{2,1,0:T(8,128)(2,1)S(1)} %bitcast.85, s32[4,1,128]{2,1,0:T(1,128)S(1)} %bitcast.86), custom_call_target="tpu_custom_call" | custom-call | tf_op jit(solution)/shard_map/exchange/pallas_call | solution.py:367
  141.4 0.8 fusion
  142.3 0.7 reshape.78
  143.0 4.1 %all-to-all-start = ((f32[8,4,16]{2,1,0:T(4,128)}), f32[8,4,16]{2,1,0:T(4,128)S(1)}, u32[]{:S(2)}, u32[]{:S(2)}) async-start(f32[8,4,16]{2,1,0:T(4,128)} %reshape.78), calls=%async_computation | async-start | bytes 32768 | tf_op jit(solution)/shard_map/all_to_all | solution.py:465
  147.0 27.8 %panel_scores.1 = f32[2,512]{1,0:T(2,128)S(1)} custom-call(bf16[512,1024]{1,0:T(8,128)(2,1)S(1)} %bitcast.84, s32[1,512]{1,0:T(1,128)S(1)} %bitcast.88, bf16[12500,1024]{1,0:T(8,128)(2,1)} %panel_ref.1), custom_call_target="tpu_custom_call" | custom-call | tf_op jit(solution)/shard_map/panel_scores/pallas_call | solution.py:238
  175.0 0.1 select_reduce_fusion
  175.1 0.6 maximum_bitcast_fusion
  175.7 3.2 %all-to-all-start.1 = ((f32[4,3,128]{2,1,0:T(4,128)}), f32[4,3,128]{2,1,0:T(4,128)S(1)}, u32[]{:S(2)}, u32[]{:S(2)}) async-start(f32[4,3,128]{2,1,0:T(4,128)} %maximum_bitcast_fusion), calls=%async_computation.1 | async-start | bytes 16384 | tf_op jit(solution)/shard_map/all_to_all | solution.py:477
  179.0 3.8 %all-to-all-done.1 = f32[4,3,128]{2,1,0:T(4,128)S(1)} async-done(((f32[4,3,128]{2,1,0:T(4,128)}), f32[4,3,128]{2,1,0:T(4,128)S(1)}, u32[]{:S(2)}, u32[]{:S(2)}) %all-to-all-start.1) | async-done | bytes 6176 | tf_op jit(solution)/shard_map/all_to_all | solution.py:477
  182.8 0.5 slice_bitcast_fusion
  183.3 0.7 copy.53
  (22 shorter events, 0.8 us)
Async XLA Ops:
  51.0 1.9 %copy-start = (bf16[128,4,16,192]{0,3,2,1:T(8,128)(2,1)S(1)}, bf16[128,4,16,192]{0,3,2,1:T(8,128)(2,1)}, u32[]{:S(2)}) copy-start(bf16[128,4,16,192]{0,3,2,1:T(8,128)(2,1)} %param.9) | copy-start | bytes 9437188
  52.9 1.0 copy-start.1
  53.9 1.0 copy-start.2
  143.0 31.9 %all-to-all-start = ((f32[8,4,16]{2,1,0:T(4,128)}), f32[8,4,16]{2,1,0:T(4,128)S(1)}, u32[]{:S(2)}, u32[]{:S(2)}) async-start(f32[8,4,16]{2,1,0:T(4,128)} %reshape.78), calls=%async_computation | async-start | bytes 32768 | tf_op jit(solution)/shard_map/all_to_all | solution.py:465
  175.7 7.0 %all-to-all-start.1 = ((f32[4,3,128]{2,1,0:T(4,128)}), f32[4,3,128]{2,1,0:T(4,128)S(1)}, u32[]{:S(2)}, u32[]{:S(2)}) async-start(f32[4,3,128]{2,1,0:T(4,128)} %maximum_bitcast_fusion), calls=%async_computation.1 | async-start | bytes 16384 | tf_op jit(solution)/shard_map/all_to_all | solution.py:477

commit v3 on v2

--- a/solution.py
+++ b/solution.py
@@ -191,7 +191,7 @@
 
 
 def score_kernel(panel_size, known, part, rows_ref, label_ref, panel_ref, out_ref, best):
-    step, final = pl.program_id(0), pl.num_programs(0) - 1
+    step = pl.program_id(0)
     tile = panel_ref.shape[0]
     rows = rows_ref.shape[0]
 
@@ -214,17 +214,9 @@
                 own = jnp.where(index == label_ref[...], scores[:known], -jnp.inf)
                 out_ref[1:2, :] = jnp.max(own, axis=0, keepdims=True)
 
-        def keep(values):
-            best[...] = jnp.maximum(best[...], jnp.max(values.reshape(part // 8, 8, rows), axis=0))
-
-        @pl.when(step < final)
-        def _():
-            keep(scores)
-
-        @pl.when(step == final)
-        def _():
-            place = step * tile + at + lax.broadcasted_iota(jnp.int32, scores.shape, 0)
-            keep(jnp.where(place < panel_size, scores, -jnp.inf))
+        place = step * tile + at + lax.broadcasted_iota(jnp.int32, scores.shape, 0)
+        scores = jnp.where(place < panel_size, scores, -jnp.inf)
+        best[...] = jnp.maximum(best[...], jnp.max(scores.reshape(part // 8, 8, rows), axis=0))
 
     @pl.when(step == pl.num_programs(0) - 1)
     def _():
@@ -417,7 +409,13 @@
     def owner_of(ids):
         return ids % panel_size % n_dp * n_cent + ids // panel_size
 
-    every_id = lax.all_gather(cluster_ids[0], both, axis=0)
+    every_id = lax.all_to_all(
+        jnp.broadcast_to(cluster_ids, (owner_total, clip_count)),
+        both,
+        split_axis=0,
+        concat_axis=0,
+        tiled=True,
+    )
     group_ids = lax.dynamic_slice_in_dim(
         every_id, lax.axis_index("dp") * n_cent, n_cent, axis=0
     ).reshape(n_cent, clip_count)

time: 184 us -> 148 us (0.80)
  blocking collectives: 43.2 us -> 0 us
  starting transfers between devices: 7.32 us -> 16.7 us
  Pallas kernels: 114 us -> 112 us
    all_gather x1 -> x0, blocking collectives: 43.2 us -> none  [local(): every_id = lax.all_gather(cluster_ids[0], both, axis=0)]
    all_to_all x0 -> x1, starting transfers between devices: none -> 7.3 us  [local(): lax.all_to_all(jnp.broadcast_to(cluster_ids, (owner_total, clip_count)),...]
    pallas_call x1, Pallas kernels: 27.8 us -> 21.8 us  [panel_scores(): pl.pallas_call(functools.partial(score_kernel, panel_size, known, part),...]
    pallas_call x1, Pallas kernels: 33.5 us -> 36.8 us  [exchange(): pl.pallas_call(functools.partial(exchange_kernel, n_dp, n_cent), out_shap...]
    all_to_all x1, starting transfers between devices: 4.07 us -> 6.19 us  [local(): lax.all_to_all(peer_values.reshape(n_dp, n_cent, capacity), 'dp', split_a...]
  transfers between devices with their start and end apart: 2 -> 3, of which waited for: 1 -> 1; matrix products, arithmetic and copies ran while one was open for 0% -> 3% of each run, Pallas kernels for 15% -> 51%
where the time goes in v3:
time: 148 us
  Pallas kernels  112 us (76%)
  starting transfers between devices  16.7 us (11%)
  local copies, waits for them, and re-layouts  9.59 us (6%)
  other arithmetic  4.3 us (3%)
  waiting for transfers between devices  3.78 us (3%)
    pallas_call x1, Pallas kernels, embed(): pl.pallas_call(embed_kernel, out_shape=jax.ShapeDtypeStruct((clips, head_...  52.9 us
    pallas_call x1, Pallas kernels, exchange(): pl.pallas_call(functools.partial(exchange_kernel, n_dp, n_cent), out_shap...  36.8 us
    pallas_call x1, Pallas kernels, panel_scores(): pl.pallas_call(functools.partial(score_kernel, panel_size, known, part),...  21.8 us
    all_to_all x1, starting transfers between devices, local(): lax.all_to_all(jnp.broadcast_to(cluster_ids, (owner_total, clip_count)),...  7.3 us
    unnamed x9, local copies, waits for them, and re-layouts  6.6 us
    all_to_all x1, starting transfers between devices, local(): lax.all_to_all(peer_values.reshape(n_dp, n_cent, capacity), 'dp', split_a...  6.19 us
    all_to_all x1, waiting for transfers between devices, local(): lax.all_to_all(partial.transpose(1, 0, 2), 'cent', split_axis=0, concat_a...  3.78 us
    all_to_all x1, starting transfers between devices, local(): lax.all_to_all(partial.transpose(1, 0, 2), 'cent', split_axis=0, concat_a...  3.25 us
  transfers between devices with their start and end apart: 3, of which 1 were waited for; matrix products, arithmetic and copies ran while one was open for 3% of the time, Pallas kernels for 51%

profile of v3, /device:TPU:0, one launch (start us, length us, event | category | flops | bytes accessed | tf_op | source)
XLA Modules:
  0.0 147.8 jit_solution(960758595889505207)
XLA Ops:
  0.6 1.3 broadcast_in_dim.103
  1.9 7.3 %all-to-all-start = ((s32[32,1,128]{2,1,0:T(1,128)}), s32[32,1,128]{2,1,0:T(1,128)S(1)}, u32[]{:S(2)}, u32[]{:S(2)}) async-start(s32[32,1,128]{2,1,0:T(1,128)} %broadcast_in_dim.103), calls=%async_computation | async-start | bytes 32768 | tf_op jit(solution)/shard_map/all_to_all | solution.py:412
  9.2 0.9 convert_reduce_fusion.1
  10.1 0.7 fusion.36
  10.8 0.8 select_reduce_fusion.2
  11.9 0.8 copy.69.depth_ref
  12.8 1.2 copy.70.reduce_ref
  14.0 1.9 %copy-done = bf16[128,4,16,192]{0,3,2,1:T(8,128)(2,1)S(1)} copy-done((bf16[128,4,16,192]{0,3,2,1:T(8,128)(2,1)S(1)}, bf16[128,4,16,192]{0,3,2,1:T(8,128)(2,1)}, u32[]{:S(2)}) %copy-start) | copy-done | bytes 3145752
  15.9 1.0 copy-done.1
  16.9 1.0 copy-done.2
  17.9 52.9 %embed_clips.1 = bf16[128,1024]{1,0:T(8,128)(2,1)S(1)} custom-call(s32[8]{0:T(128)S(1)} %slice.3.most_ref, s32[128,1]{1,0:T(8,128)S(1)} %copy.67.order_ref, bf16[4,16,192,128]{3,2,1,0:T(8,128)(2,1)S(1)} %bitcast.92, f32[128,1]{1,0:T(8,128)S(1)} %copy.68.count_ref, s32[1,128]{1,0:T(1,128)S(1)} %bitcast.96, bf16[2,192,432]{2,1,0:T(8,128)(2,1)S(1)} %copy-done.1, ...), custom_call_target="tpu_custom_call" | custom-call | tf_op jit(solution)/shard_map/embed_clips/pallas_call | solution.py:166
  70.9 0.2 convolution_convert_fusion
  71.1 0.2 compare_select_fusion.2
  71.4 0.6 select_reduce_fusion.1
  72.3 36.8 %exchange.1 = (bf16[128,1024]{1,0:T(8,128)(2,1)S(1)}, bf16[4,128,1024]{2,1,0:T(8,128)(2,1)S(1)}, bf16[8,4,16,1024]{3,2,1,0:T(8,128)(2,1)S(1)}) custom-call(bf16[8,16,1024]{2,1,0:T(8,128)(2,1)S(1)} %bitcast.94, s32[4,1,128]{2,1,0:T(1,128)S(1)} %copy_select_fusion.2.seat_ref), custom_call_target="tpu_custom_call" | custom-call | tf_op jit(solution)/shard_map/exchange/pallas_call | solution.py:359
  109.1 0.8 fusion
  110.0 0.7 reshape.143
  110.7 6.2 %all-to-all-start.1 = ((f32[8,4,16]{2,1,0:T(4,128)}), f32[8,4,16]{2,1,0:T(4,128)S(1)}, u32[]{:S(2)}, u32[]{:S(2)}) async-start(f32[8,4,16]{2,1,0:T(4,128)} %reshape.143), calls=%async_computation.1 | async-start | bytes 32768 | tf_op jit(solution)/shard_map/all_to_all | solution.py:463
  116.9 21.8 %panel_scores.1 = f32[2,512]{1,0:T(2,128)S(1)} custom-call(bf16[512,1024]{1,0:T(8,128)(2,1)S(1)} %bitcast.93, s32[1,512]{1,0:T(1,128)S(1)} %get-tuple-element.13.label_ref, bf16[12500,1024]{1,0:T(8,128)(2,1)} %panel_ref.1), custom_call_target="tpu_custom_call" | custom-call | tf_op jit(solution)/shard_map/panel_scores/pallas_call | solution.py:230
  138.9 0.6 maximum_bitcast_fusion
  139.5 3.2 %all-to-all-start.2 = ((f32[4,3,128]{2,1,0:T(4,128)}), f32[4,3,128]{2,1,0:T(4,128)S(1)}, u32[]{:S(2)}, u32[]{:S(2)}) async-start(f32[4,3,128]{2,1,0:T(4,128)} %maximum_bitcast_fusion), calls=%async_computation.2 | async-start | bytes 16384 | tf_op jit(solution)/shard_map/all_to_all | solution.py:475
  142.8 3.8 %all-to-all-done.2 = f32[4,3,128]{2,1,0:T(4,128)S(1)} async-done(((f32[4,3,128]{2,1,0:T(4,128)}), f32[4,3,128]{2,1,0:T(4,128)S(1)}, u32[]{:S(2)}, u32[]{:S(2)}) %all-to-all-start.2) | async-done | bytes 6176 | tf_op jit(solution)/shard_map/all_to_all | solution.py:475
  146.5 0.5 slice_bitcast_fusion
  147.1 0.7 copy.105
  (31 shorter events, 1.0 us)
Async XLA Ops:
  1.9 68.9 %all-to-all-start = ((s32[32,1,128]{2,1,0:T(1,128)}), s32[32,1,128]{2,1,0:T(1,128)S(1)}, u32[]{:S(2)}, u32[]{:S(2)}) async-start(s32[32,1,128]{2,1,0:T(1,128)} %broadcast_in_dim.103), calls=%async_computation | async-start | bytes 32768 | tf_op jit(solution)/shard_map/all_to_all | solution.py:412
  14.0 1.9 %copy-start = (bf16[128,4,16,192]{0,3,2,1:T(8,128)(2,1)S(1)}, bf16[128,4,16,192]{0,3,2,1:T(8,128)(2,1)}, u32[]{:S(2)}) copy-start(bf16[128,4,16,192]{0,3,2,1:T(8,128)(2,1)} %param.9) | copy-start | bytes 9437188
  15.9 1.0 copy-start.1
  16.9 1.0 copy-start.2
  110.7 28.0 %all-to-all-start.1 = ((f32[8,4,16]{2,1,0:T(4,128)}), f32[8,4,16]{2,1,0:T(4,128)S(1)}, u32[]{:S(2)}, u32[]{:S(2)}) async-start(f32[8,4,16]{2,1,0:T(4,128)} %reshape.143), calls=%async_computation.1 | async-start | bytes 32768 | tf_op jit(solution)/shard_map/all_to_all | solution.py:463
  139.5 7.0 %all-to-all-start.2 = ((f32[4,3,128]{2,1,0:T(4,128)}), f32[4,3,128]{2,1,0:T(4,128)S(1)}, u32[]{:S(2)}, u32[]{:S(2)}) async-start(f32[4,3,128]{2,1,0:T(4,128)} %maximum_bitcast_fusion), calls=%async_computation.2 | async-start | bytes 16384 | tf_op jit(solution)/shard_map/all_to_all | solution.py:475
